TPU v7x, 256 devices: a whole 4x4x8 slice. The times are simulated.
256 devices in a mesh: rows: 64 (over z, y_hi, x), rep: 4 (over y_lo, core).
Axes of the slice: x: 4, y: 4 (y_hi: 2, y_lo: 2; y = y_hi * 2 + y_lo), z: 8, core: 2. Of those that a mesh axis runs over, the one named last changes fastest.
Arguments:
- features: bfloat16 [49152, 256], P('rows'), may hold values from -6 to 6
- degrees: int32 [49152], P('rows'), may hold values from 1 to 8
- cotangent: bfloat16 [49152, 256], P('rows'), may hold values from -6 to 6
- self_weight: bfloat16 [256, 256], replicated, may hold values from -0.375 to 0.375
- neigh_weight: bfloat16 [256, 256], replicated, may hold values from -0.375 to 0.375
- bias_vector: bfloat16 [256], replicated, may hold values from -3 to 3
- block_values: bfloat16 [64, 64, 12, 128, 128], P('rows', 'rep'), may hold values from -0.14941406 to 0.14941406
- block_rows: int32 [64, 64, 12], P('rows', 'rep'), may hold values from 0 to 5
- block_cols: int32 [64, 64, 12], P('rows', 'rep'), may hold values from 0 to 5
- block_count: int32 [64, 64], P('rows', 'rep'), may hold values from 1 to 12, as said below
Outputs:
- output: bfloat16 [49152, 256], P(('rows', 'rep'))
- grad_input: bfloat16 [49152, 256], P(('rows', 'rep'))
Inputs may be any that keep to these rules, and one draw needn't show every extreme that they name: block_count[p, d] is the number of live slots of row panel p at distance d; some pair holds 12 in every draw.
All inputs are finite; a program needn't handle non-finite values.
Results may differ from a plain program's by a relative error of at most 0.012.
Values may be sent and summed in bfloat16 or wider, within the bound.
A program may use at most 192 MiB of HBM per device.

v0:
```python
import jax
import jax.numpy as jnp
from jax import lax
from jax.sharding import PartitionSpec as P


def passed_along(block, axis, distance):
    devices = range(lax.axis_size(axis))
    route = [((i - distance) % len(devices), i) for i in devices]
    return lax.ppermute(block, axis, route)


def silu_slope(preact):
    sigmoid_value = jax.nn.sigmoid(preact)
    return sigmoid_value * (1.0 + preact * (1.0 - sigmoid_value))


def move_panel(current, offset):
    return passed_along(current, "rows", offset)


def move_partial(running, offset):
    return passed_along(running, "rows", offset)


def select_bit(shifted, unshifted, replica, bit_level):
    return jnp.where(replica // (1 << bit_level) % 2 == 1, shifted, unshifted)


def padded_blocks(source3, weights, source_ids, target_ids, count_here, transpose):
    picked = jnp.take(source3, source_ids, axis=0)
    pattern = "kji,kjf->kif" if transpose else "kij,kjf->kif"
    product = jnp.einsum(pattern, weights, picked, preferred_element_type=jnp.float32)
    slot_ids = jnp.arange(weights.shape[0], dtype=jnp.int32)
    block_ids = jnp.arange(source3.shape[0], dtype=jnp.int32)
    placement = (
        (target_ids[None, :] == block_ids[:, None]) & (slot_ids < count_here)[None, :]
    ).astype(jnp.float32)
    return jnp.einsum("rk,kif->rif", placement, product, precision=lax.Precision.HIGHEST)


def section_blocks(source3, weights, source_ids, target_ids, count_here, transpose):
    return padded_blocks(source3, weights, source_ids, target_ids, count_here, transpose)


def on_device(
    features,
    degrees,
    cotangent,
    self_weight,
    neigh_weight,
    bias_vector,
    block_values,
    block_rows,
    block_cols,
    block_count,
):
    replicas = lax.axis_size("rep")
    sections = lax.axis_size("rows") // replicas
    replica = lax.axis_index("rep")
    feature_width = features.shape[1]
    block_size = block_values.shape[-1]
    panel_rows = features.shape[0]
    row_blocks = panel_rows // block_size
    quarter = panel_rows // replicas
    first_row = replica * quarter
    weights_all = block_values[0]
    rows_all = block_rows[0]
    cols_all = block_cols[0]
    counts_all = block_count[0]
    final_section = sections - 1
    current = features.reshape(row_blocks, block_size, feature_width)
    for bit_level in range(replicas.bit_length() - 1):
        current = select_bit(
            move_panel(current, sections << bit_level), current, replica, bit_level
        )

    def forward_section(section_index, carried):
        running, panel_now = carried
        running = running + section_blocks(
            panel_now,
            weights_all[section_index],
            cols_all[section_index],
            rows_all[section_index],
            counts_all[section_index],
            False,
        )
        return (running, move_panel(panel_now, 1))

    initial = jnp.zeros((row_blocks, block_size, feature_width), jnp.float32)
    running, current = lax.fori_loop(0, sections - 1, forward_section, (initial, current))
    running = running + section_blocks(
        current,
        weights_all[final_section],
        cols_all[final_section],
        rows_all[final_section],
        counts_all[final_section],
        False,
    )
    partial_agg = running.reshape(panel_rows, feature_width)

    def own_rows(source):
        return lax.dynamic_slice_in_dim(source, first_row, quarter, 0)

    summed = lax.psum(partial_agg, "rep")
    divisor = degrees.astype(jnp.float32)[:, None]
    neighbours = (summed / divisor).astype(jnp.bfloat16)
    preact = jnp.dot(features, self_weight, preferred_element_type=jnp.float32)
    preact = preact + jnp.dot(neighbours, neigh_weight, preferred_element_type=jnp.float32)
    preact = preact + bias_vector.astype(jnp.float32)[None, :]
    activated = jax.nn.silu(preact).astype(jnp.bfloat16)
    pre_grad = (cotangent.astype(jnp.float32) * silu_slope(preact)).astype(jnp.bfloat16)
    scaled = (
        jnp.dot(pre_grad, neigh_weight.T, preferred_element_type=jnp.float32) / divisor
    ).astype(jnp.bfloat16)
    activated, pre_grad, scaled = (activated, pre_grad, scaled)
    output = own_rows(activated)
    grad_rows = own_rows(pre_grad)
    scaled3 = scaled.reshape(row_blocks, block_size, feature_width)

    def backward_one(weights, rows_here, cols_here, count_here):
        return section_blocks(scaled3, weights, rows_here, cols_here, count_here, True)

    def backward_section(step_index, running_back):
        section_index = sections - 2 - step_index
        arrived = move_partial(running_back, -1)
        return arrived + backward_one(
            weights_all[section_index],
            rows_all[section_index],
            cols_all[section_index],
            counts_all[section_index],
        )

    first_back = backward_one(
        weights_all[final_section],
        rows_all[final_section],
        cols_all[final_section],
        counts_all[final_section],
    )
    returned = lax.fori_loop(0, sections - 1, backward_section, first_back)
    for bit_level in range(replicas.bit_length() - 1):
        returned = select_bit(
            move_partial(returned, -(sections << bit_level)), returned, replica, bit_level
        )
    back_part = lax.psum_scatter(
        returned.reshape(panel_rows, feature_width).astype(jnp.bfloat16),
        "rep",
        scatter_dimension=0,
        tiled=True,
    ).astype(jnp.float32)
    grad_input = jnp.dot(grad_rows, self_weight.T, preferred_element_type=jnp.float32) + back_part
    return (output, grad_input.astype(jnp.bfloat16))


def solution(mesh):
    return jax.shard_map(
        on_device,
        mesh=mesh,
        in_specs=(
            P("rows", None),
            P("rows"),
            P("rows", None),
            P(),
            P(),
            P(),
            P("rows", "rep", None, None, None),
            P("rows", "rep", None),
            P("rows", "rep", None),
            P("rows", "rep"),
        ),
        out_specs=(P(("rows", "rep"), None), P(("rows", "rep"), None)),
        check_vma=False,
    )
```

profile of v0, /device:TPU:1, one launch (start us, length us, event | category | flops | bytes accessed | tf_op | source)
XLA Modules:
  0.0 775.7 jit_solution(9083673453901701395)
XLA Ops:
  16.1 10.1 %collective-permute-done.2 = bf16[6,128,256]{2,1,0:T(8,128)(2,1)S(1)} collective-permute-done((bf16[6,128,256]{2,1,0:T(8,128)(2,1)}, bf16[6,128,256]{2,1,0:T(8,128)(2,1)S(1)}, u32[]{:S(2)}, u32[]{:S(2)}) %collective-permute-start.2) | collective-permute-done | bytes 393248 | tf_op jit(solution)/shard_map/ppermute | solution.py:10
  26.2 10.2 %collective-permute-start.3 = (bf16[6,128,256]{2,1,0:T(8,128)(2,1)S(1)}, bf16[6,128,256]{2,1,0:T(8,128)(2,1)S(1)}, u32[]{:S(2)}, u32[]{:S(2)}) collective-permute-start(bf16[6,128,256]{2,1,0:T(8,128)(2,1)S(1)} %broadcast_select_fusion.1), channel_id=1, source_target_pairs={{128,0},{132,4},{136,8},{140,12},{144,16},{148,20},{152,24},{156,2... | collective-permute-start | bytes 1179656 | tf_op jit(solution)/shard_map/ppermute | solution.py:10
  37.1 16.5 %collective-permute-done.3 = bf16[6,128,256]{2,1,0:T(8,128)(2,1)S(1)} collective-permute-done((bf16[6,128,256]{2,1,0:T(8,128)(2,1)S(1)}, bf16[6,128,256]{2,1,0:T(8,128)(2,1)S(1)}, u32[]{:S(2)}, u32[]{:S(2)}) %collective-permute-start.3) | collective-permute-done | bytes 393248 | tf_op jit(solution)/shard_map/ppermute | solution.py:10
  53.6 211.7 %while.32 = (s32[]{:T(128)}, f32[6,128,256]{2,0,1:T(8,128)S(1)}, bf16[6,128,256]{2,1,0:T(8,128)(2,1)S(1)}, s32[16,12]{1,0:T(8,128)S(1)}, s32[16]{0:T(128)S(1)}, ...) while((s32[]{:T(128)}, f32[6,128,256]{2,0,1:T(8,128)S(1)}, ...), condition=%wide.region_1.3_spmd.clone, body=%wide.region_0.2_spmd.clone.sunk | while | flops 129762528 | bytes 9835059 | solution.py:91
  60.4 9.1 %collective-permute-done.1 = bf16[6,128,256]{2,1,0:T(8,128)(2,1)S(1)} collective-permute-done((bf16[6,128,256]{2,1,0:T(8,128)(2,1)S(1)}, bf16[6,128,256]{2,1,0:T(8,128)(2,1)S(1)}, u32[]{:S(2)}, u32[]{:S(2)}) %collective-permute-start.1) | collective-permute-done | bytes 393248 | tf_op jit(solution)/shard_map/while/body/eval_jaxpr/ppermute | solution.py:10
  75.1 9.3 %collective-permute-done.1 = bf16[6,128,256]{2,1,0:T(8,128)(2,1)S(1)} collective-permute-done((bf16[6,128,256]{2,1,0:T(8,128)(2,1)S(1)}, bf16[6,128,256]{2,1,0:T(8,128)(2,1)S(1)}, u32[]{:S(2)}, u32[]{:S(2)}) %collective-permute-start.1) | collective-permute-done | bytes 393248 | tf_op jit(solution)/shard_map/while/body/eval_jaxpr/ppermute | solution.py:10
  90.0 8.4 %collective-permute-done.1 = bf16[6,128,256]{2,1,0:T(8,128)(2,1)S(1)} collective-permute-done((bf16[6,128,256]{2,1,0:T(8,128)(2,1)S(1)}, bf16[6,128,256]{2,1,0:T(8,128)(2,1)S(1)}, u32[]{:S(2)}, u32[]{:S(2)}) %collective-permute-start.1) | collective-permute-done | bytes 393248 | tf_op jit(solution)/shard_map/while/body/eval_jaxpr/ppermute | solution.py:10
  104.0 7.5 collective-permute-done.1
  117.1 6.9 collective-permute-done.1
  129.5 6.9 collective-permute-done.1
  142.0 6.9 collective-permute-done.1
  154.5 6.9 collective-permute-done.1
  166.9 6.9 collective-permute-done.1
  179.4 8.0 %collective-permute-done.1 = bf16[6,128,256]{2,1,0:T(8,128)(2,1)S(1)} collective-permute-done((bf16[6,128,256]{2,1,0:T(8,128)(2,1)S(1)}, bf16[6,128,256]{2,1,0:T(8,128)(2,1)S(1)}, u32[]{:S(2)}, u32[]{:S(2)}) %collective-permute-start.1) | collective-permute-done | bytes 393248 | tf_op jit(solution)/shard_map/while/body/eval_jaxpr/ppermute | solution.py:10
  192.9 9.0 %collective-permute-done.1 = bf16[6,128,256]{2,1,0:T(8,128)(2,1)S(1)} collective-permute-done((bf16[6,128,256]{2,1,0:T(8,128)(2,1)S(1)}, bf16[6,128,256]{2,1,0:T(8,128)(2,1)S(1)}, u32[]{:S(2)}, u32[]{:S(2)}) %collective-permute-start.1) | collective-permute-done | bytes 393248 | tf_op jit(solution)/shard_map/while/body/eval_jaxpr/ppermute | solution.py:10
  207.6 10.1 %collective-permute-done.1 = bf16[6,128,256]{2,1,0:T(8,128)(2,1)S(1)} collective-permute-done((bf16[6,128,256]{2,1,0:T(8,128)(2,1)S(1)}, bf16[6,128,256]{2,1,0:T(8,128)(2,1)S(1)}, u32[]{:S(2)}, u32[]{:S(2)}) %collective-permute-start.1) | collective-permute-done | bytes 393248 | tf_op jit(solution)/shard_map/while/body/eval_jaxpr/ppermute | solution.py:10
  223.3 11.2 %collective-permute-done.1 = bf16[6,128,256]{2,1,0:T(8,128)(2,1)S(1)} collective-permute-done((bf16[6,128,256]{2,1,0:T(8,128)(2,1)S(1)}, bf16[6,128,256]{2,1,0:T(8,128)(2,1)S(1)}, u32[]{:S(2)}, u32[]{:S(2)}) %collective-permute-start.1) | collective-permute-done | bytes 393248 | tf_op jit(solution)/shard_map/while/body/eval_jaxpr/ppermute | solution.py:10
  240.0 10.3 %collective-permute-done.1 = bf16[6,128,256]{2,1,0:T(8,128)(2,1)S(1)} collective-permute-done((bf16[6,128,256]{2,1,0:T(8,128)(2,1)S(1)}, bf16[6,128,256]{2,1,0:T(8,128)(2,1)S(1)}, u32[]{:S(2)}, u32[]{:S(2)}) %collective-permute-start.1) | collective-permute-done | bytes 393248 | tf_op jit(solution)/shard_map/while/body/eval_jaxpr/ppermute | solution.py:10
  256.0 9.4 %collective-permute-done.1 = bf16[6,128,256]{2,1,0:T(8,128)(2,1)S(1)} collective-permute-done((bf16[6,128,256]{2,1,0:T(8,128)(2,1)S(1)}, bf16[6,128,256]{2,1,0:T(8,128)(2,1)S(1)}, u32[]{:S(2)}, u32[]{:S(2)}) %collective-permute-start.1) | collective-permute-done | bytes 393248 | tf_op jit(solution)/shard_map/while/body/eval_jaxpr/ppermute | solution.py:10
  273.7 57.4 %all-reduce.2.cloned.1.call-done = f32[768,256]{1,0:T(8,128)} async-done(((f32[768,256]{1,0:T(8,128)}), f32[768,256]{1,0:T(8,128)}) %all-reduce.2.cloned.1.call-update) | async-done | bytes 786448 | tf_op jit(solution)/shard_map/psum | solution.py:105
  341.0 353.0 %while.31 = (s32[]{:T(128)}, f32[6,128,256]{2,0,1:T(8,128)S(1)}, s32[16,12]{1,0:T(8,128)S(1)}, s32[16]{0:T(128)S(1)}, bf16[16,12,128,128]{3,2,1,0:T(8,128)(2,1)}...) while((s32[]{:T(128)}, f32[6,128,256]{2,0,1:T(8,128)S(1)}, ...), condition=%wide.region_4.6_spmd, body=%wide.region_3.5_spmd.sunk | while | flops 129565936 | bytes 12194407 | solution.py:140
  342.1 7.3 collective-permute-start
  352.8 13.8 %collective-permute-done = f32[6,128,256]{2,1,0:T(8,128)S(1)} collective-permute-done((f32[6,128,256]{2,1,0:T(8,128)}, f32[6,128,256]{2,1,0:T(8,128)S(1)}, u32[]{:S(2)}, u32[]{:S(2)}) %collective-permute-start) | collective-permute-done | bytes 786464 | tf_op jit(solution)/shard_map/while/body/eval_jaxpr/ppermute | solution.py:10
  369.8 7.8 %collective-permute-start = (f32[6,128,256]{2,1,0:T(8,128)}, f32[6,128,256]{2,1,0:T(8,128)S(1)}, u32[]{:S(2)}, u32[]{:S(2)}) collective-permute-start(f32[6,128,256]{2,1,0:T(8,128)} %copy.54), channel_id=1, source_target_pairs={{4,0},{8,4},{12,8},{16,12},{20,16},{24,20},{28,24},{32,28},{36,32}... | collective-permute-start | bytes 2359304 | tf_op jit(solution)/shard_map/while/body/eval_jaxpr/ppermute | solution.py:10
  381.0 12.9 %collective-permute-done = f32[6,128,256]{2,1,0:T(8,128)S(1)} collective-permute-done((f32[6,128,256]{2,1,0:T(8,128)}, f32[6,128,256]{2,1,0:T(8,128)S(1)}, u32[]{:S(2)}, u32[]{:S(2)}) %collective-permute-start) | collective-permute-done | bytes 786464 | tf_op jit(solution)/shard_map/while/body/eval_jaxpr/ppermute | solution.py:10
  397.1 7.8 %collective-permute-start = (f32[6,128,256]{2,1,0:T(8,128)}, f32[6,128,256]{2,1,0:T(8,128)S(1)}, u32[]{:S(2)}, u32[]{:S(2)}) collective-permute-start(f32[6,128,256]{2,1,0:T(8,128)} %copy.54), channel_id=1, source_target_pairs={{4,0},{8,4},{12,8},{16,12},{20,16},{24,20},{28,24},{32,28},{36,32}... | collective-permute-start | bytes 2359304 | tf_op jit(solution)/shard_map/while/body/eval_jaxpr/ppermute | solution.py:10
  408.2 11.9 %collective-permute-done = f32[6,128,256]{2,1,0:T(8,128)S(1)} collective-permute-done((f32[6,128,256]{2,1,0:T(8,128)}, f32[6,128,256]{2,1,0:T(8,128)S(1)}, u32[]{:S(2)}, u32[]{:S(2)}) %collective-permute-start) | collective-permute-done | bytes 786464 | tf_op jit(solution)/shard_map/while/body/eval_jaxpr/ppermute | solution.py:10
  423.4 7.8 %collective-permute-start = (f32[6,128,256]{2,1,0:T(8,128)}, f32[6,128,256]{2,1,0:T(8,128)S(1)}, u32[]{:S(2)}, u32[]{:S(2)}) collective-permute-start(f32[6,128,256]{2,1,0:T(8,128)} %copy.54), channel_id=1, source_target_pairs={{4,0},{8,4},{12,8},{16,12},{20,16},{24,20},{28,24},{32,28},{36,32}... | collective-permute-start | bytes 2359304 | tf_op jit(solution)/shard_map/while/body/eval_jaxpr/ppermute | solution.py:10
  434.6 11.0 %collective-permute-done = f32[6,128,256]{2,1,0:T(8,128)S(1)} collective-permute-done((f32[6,128,256]{2,1,0:T(8,128)}, f32[6,128,256]{2,1,0:T(8,128)S(1)}, u32[]{:S(2)}, u32[]{:S(2)}) %collective-permute-start) | collective-permute-done | bytes 786464 | tf_op jit(solution)/shard_map/while/body/eval_jaxpr/ppermute | solution.py:10
  448.8 7.8 %collective-permute-start = (f32[6,128,256]{2,1,0:T(8,128)}, f32[6,128,256]{2,1,0:T(8,128)S(1)}, u32[]{:S(2)}, u32[]{:S(2)}) collective-permute-start(f32[6,128,256]{2,1,0:T(8,128)} %copy.54), channel_id=1, source_target_pairs={{4,0},{8,4},{12,8},{16,12},{20,16},{24,20},{28,24},{32,28},{36,32}... | collective-permute-start | bytes 2359304 | tf_op jit(solution)/shard_map/while/body/eval_jaxpr/ppermute | solution.py:10
  460.0 10.1 %collective-permute-done = f32[6,128,256]{2,1,0:T(8,128)S(1)} collective-permute-done((f32[6,128,256]{2,1,0:T(8,128)}, f32[6,128,256]{2,1,0:T(8,128)S(1)}, u32[]{:S(2)}, u32[]{:S(2)}) %collective-permute-start) | collective-permute-done | bytes 786464 | tf_op jit(solution)/shard_map/while/body/eval_jaxpr/ppermute | solution.py:10
  473.3 7.8 %collective-permute-start = (f32[6,128,256]{2,1,0:T(8,128)}, f32[6,128,256]{2,1,0:T(8,128)S(1)}, u32[]{:S(2)}, u32[]{:S(2)}) collective-permute-start(f32[6,128,256]{2,1,0:T(8,128)} %copy.54), channel_id=1, source_target_pairs={{4,0},{8,4},{12,8},{16,12},{20,16},{24,20},{28,24},{32,28},{36,32}... | collective-permute-start | bytes 2359304 | tf_op jit(solution)/shard_map/while/body/eval_jaxpr/ppermute | solution.py:10
  484.5 9.2 %collective-permute-done = f32[6,128,256]{2,1,0:T(8,128)S(1)} collective-permute-done((f32[6,128,256]{2,1,0:T(8,128)}, f32[6,128,256]{2,1,0:T(8,128)S(1)}, u32[]{:S(2)}, u32[]{:S(2)}) %collective-permute-start) | collective-permute-done | bytes 786464 | tf_op jit(solution)/shard_map/while/body/eval_jaxpr/ppermute | solution.py:10
  496.9 7.8 %collective-permute-start = (f32[6,128,256]{2,1,0:T(8,128)}, f32[6,128,256]{2,1,0:T(8,128)S(1)}, u32[]{:S(2)}, u32[]{:S(2)}) collective-permute-start(f32[6,128,256]{2,1,0:T(8,128)} %copy.54), channel_id=1, source_target_pairs={{4,0},{8,4},{12,8},{16,12},{20,16},{24,20},{28,24},{32,28},{36,32}... | collective-permute-start | bytes 2359304 | tf_op jit(solution)/shard_map/while/body/eval_jaxpr/ppermute | solution.py:10
  508.0 8.3 %collective-permute-done = f32[6,128,256]{2,1,0:T(8,128)S(1)} collective-permute-done((f32[6,128,256]{2,1,0:T(8,128)}, f32[6,128,256]{2,1,0:T(8,128)S(1)}, u32[]{:S(2)}, u32[]{:S(2)}) %collective-permute-start) | collective-permute-done | bytes 786464 | tf_op jit(solution)/shard_map/while/body/eval_jaxpr/ppermute | solution.py:10
  519.5 7.8 %collective-permute-start = (f32[6,128,256]{2,1,0:T(8,128)}, f32[6,128,256]{2,1,0:T(8,128)S(1)}, u32[]{:S(2)}, u32[]{:S(2)}) collective-permute-start(f32[6,128,256]{2,1,0:T(8,128)} %copy.54), channel_id=1, source_target_pairs={{4,0},{8,4},{12,8},{16,12},{20,16},{24,20},{28,24},{32,28},{36,32}... | collective-permute-start | bytes 2359304 | tf_op jit(solution)/shard_map/while/body/eval_jaxpr/ppermute | solution.py:10
  530.7 7.3 collective-permute-done
  541.3 7.8 %collective-permute-start = (f32[6,128,256]{2,1,0:T(8,128)}, f32[6,128,256]{2,1,0:T(8,128)S(1)}, u32[]{:S(2)}, u32[]{:S(2)}) collective-permute-start(f32[6,128,256]{2,1,0:T(8,128)} %copy.54), channel_id=1, source_target_pairs={{4,0},{8,4},{12,8},{16,12},{20,16},{24,20},{28,24},{32,28},{36,32}... | collective-permute-start | bytes 2359304 | tf_op jit(solution)/shard_map/while/body/eval_jaxpr/ppermute | solution.py:10
  562.1 7.8 %collective-permute-start = (f32[6,128,256]{2,1,0:T(8,128)}, f32[6,128,256]{2,1,0:T(8,128)S(1)}, u32[]{:S(2)}, u32[]{:S(2)}) collective-permute-start(f32[6,128,256]{2,1,0:T(8,128)} %copy.54), channel_id=1, source_target_pairs={{4,0},{8,4},{12,8},{16,12},{20,16},{24,20},{28,24},{32,28},{36,32}... | collective-permute-start | bytes 2359304 | tf_op jit(solution)/shard_map/while/body/eval_jaxpr/ppermute | solution.py:10
  582.4 7.5 collective-permute-start
  602.4 7.5 collective-permute-start
  622.4 7.5 collective-permute-start
  642.5 7.5 collective-permute-start
  663.1 7.5 collective-permute-start
  674.0 17.9 %collective-permute-done = f32[6,128,256]{2,1,0:T(8,128)S(1)} collective-permute-done((f32[6,128,256]{2,1,0:T(8,128)}, f32[6,128,256]{2,1,0:T(8,128)S(1)}, u32[]{:S(2)}, u32[]{:S(2)}) %collective-permute-start) | collective-permute-done | bytes 786464 | tf_op jit(solution)/shard_map/while/body/eval_jaxpr/ppermute | solution.py:10
  694.3 20.4 %collective-permute-done.4 = bf16[6,128,256]{2,1,0:T(8,128)(2,1)S(1)} collective-permute-done((bf16[6,128,256]{2,1,0:T(8,128)(2,1)S(1)}, bf16[6,128,256]{2,1,0:T(8,128)(2,1)S(1)}, u32[]{:S(2)}, u32[]{:S(2)}) %collective-permute-start.4) | collective-permute-done | bytes 393248 | tf_op jit(solution)/shard_map/ppermute | solution.py:10
  715.0 7.1 collective-permute-start.5
  732.4 34.9 %reduce-scatter.2.cloned.1.call-done = bf16[192,256]{1,0:T(8,128)(2,1)} async-done(((bf16[768,256]{1,0:T(8,128)(2,1)}), bf16[192,256]{1,0:T(8,128)(2,1)}) %reduce-scatter.2.cloned.1.call-update) | async-done | bytes 98320 | tf_op jit(solution)/shard_map/reduce_scatter | solution.py:145
  (348 shorter events, 258.4 us)
Async XLA Ops:
  7.2 323.8 %copy-start = (bf16[256,256]{1,0:T(8,128)(2,1)S(1)}, bf16[256,256]{1,0:T(8,128)(2,1)}, u32[]{:S(2)}) copy-start(bf16[256,256]{1,0:T(8,128)(2,1)} %param.20) | copy-start | bytes 393220
  7.2 46.4 %copy-start.7 = (s32[1,16]{1,0:T(1,128)S(1)}, s32[1,16]{1,0:T(1,128)}, u32[]{:S(2)}) copy-start(s32[1,16]{1,0:T(1,128)} %param.25) | copy-start | bytes 196
  7.2 323.8 %all-reduce.2.cloned.1.call-start = ((), (), s32[]{:S(2)}) async-start(), calls=%async_computation.1 | async-start | bytes 1572864 | tf_op jit(solution)/shard_map/psum | solution.py:105
  7.2 19.0 %collective-permute-start.2 = (bf16[6,128,256]{2,1,0:T(8,128)(2,1)}, bf16[6,128,256]{2,1,0:T(8,128)(2,1)S(1)}, u32[]{:S(2)}, u32[]{:S(2)}) collective-permute-start(bf16[6,128,256]{2,1,0:T(8,128)(2,1)} %bitcast.86), channel_id=1, source_target_pairs={{192,0},{196,4},{200,8},{204,12},{208,16},{212,20},{216,24},{220,2... | collective-permute-start | bytes 1179656 | tf_op jit(solution)/shard_map/ppermute | solution.py:10
  26.2 27.3 %collective-permute-start.3 = (bf16[6,128,256]{2,1,0:T(8,128)(2,1)S(1)}, bf16[6,128,256]{2,1,0:T(8,128)(2,1)S(1)}, u32[]{:S(2)}, u32[]{:S(2)}) collective-permute-start(bf16[6,128,256]{2,1,0:T(8,128)(2,1)S(1)} %broadcast_select_fusion.1), channel_id=1, source_target_pairs={{128,0},{132,4},{136,8},{140,12},{144,16},{148,20},{152,24},{156,2... | collective-permute-start | bytes 1179656 | tf_op jit(solution)/shard_map/ppermute | solution.py:10
  53.7 15.8 %collective-permute-start.1 = (bf16[6,128,256]{2,1,0:T(8,128)(2,1)S(1)}, bf16[6,128,256]{2,1,0:T(8,128)(2,1)S(1)}, u32[]{:S(2)}, u32[]{:S(2)}) collective-permute-start(bf16[6,128,256]{2,1,0:T(8,128)(2,1)S(1)} %copy.61), channel_id=1, source_target_pairs={{252,0},{0,4},{4,8},{8,12},{12,16},{16,20},{20,24},{24,28},{28,32}... | collective-permute-start | bytes 1179656 | tf_op jit(solution)/shard_map/while/body/eval_jaxpr/ppermute | solution.py:10
  69.5 14.9 %collective-permute-start.1 = (bf16[6,128,256]{2,1,0:T(8,128)(2,1)S(1)}, bf16[6,128,256]{2,1,0:T(8,128)(2,1)S(1)}, u32[]{:S(2)}, u32[]{:S(2)}) collective-permute-start(bf16[6,128,256]{2,1,0:T(8,128)(2,1)S(1)} %copy.61), channel_id=1, source_target_pairs={{252,0},{0,4},{4,8},{8,12},{12,16},{16,20},{20,24},{24,28},{28,32}... | collective-permute-start | bytes 1179656 | tf_op jit(solution)/shard_map/while/body/eval_jaxpr/ppermute | solution.py:10
  84.4 14.0 %collective-permute-start.1 = (bf16[6,128,256]{2,1,0:T(8,128)(2,1)S(1)}, bf16[6,128,256]{2,1,0:T(8,128)(2,1)S(1)}, u32[]{:S(2)}, u32[]{:S(2)}) collective-permute-start(bf16[6,128,256]{2,1,0:T(8,128)(2,1)S(1)} %copy.61), channel_id=1, source_target_pairs={{252,0},{0,4},{4,8},{8,12},{12,16},{16,20},{20,24},{24,28},{28,32}... | collective-permute-start | bytes 1179656 | tf_op jit(solution)/shard_map/while/body/eval_jaxpr/ppermute | solution.py:10
  98.5 13.1 %collective-permute-start.1 = (bf16[6,128,256]{2,1,0:T(8,128)(2,1)S(1)}, bf16[6,128,256]{2,1,0:T(8,128)(2,1)S(1)}, u32[]{:S(2)}, u32[]{:S(2)}) collective-permute-start(bf16[6,128,256]{2,1,0:T(8,128)(2,1)S(1)} %copy.61), channel_id=1, source_target_pairs={{252,0},{0,4},{4,8},{8,12},{12,16},{16,20},{20,24},{24,28},{28,32}... | collective-permute-start | bytes 1179656 | tf_op jit(solution)/shard_map/while/body/eval_jaxpr/ppermute | solution.py:10
  111.5 12.4 %collective-permute-start.1 = (bf16[6,128,256]{2,1,0:T(8,128)(2,1)S(1)}, bf16[6,128,256]{2,1,0:T(8,128)(2,1)S(1)}, u32[]{:S(2)}, u32[]{:S(2)}) collective-permute-start(bf16[6,128,256]{2,1,0:T(8,128)(2,1)S(1)} %copy.61), channel_id=1, source_target_pairs={{252,0},{0,4},{4,8},{8,12},{12,16},{16,20},{20,24},{24,28},{28,32}... | collective-permute-start | bytes 1179656 | tf_op jit(solution)/shard_map/while/body/eval_jaxpr/ppermute | solution.py:10
  124.0 12.4 %collective-permute-start.1 = (bf16[6,128,256]{2,1,0:T(8,128)(2,1)S(1)}, bf16[6,128,256]{2,1,0:T(8,128)(2,1)S(1)}, u32[]{:S(2)}, u32[]{:S(2)}) collective-permute-start(bf16[6,128,256]{2,1,0:T(8,128)(2,1)S(1)} %copy.61), channel_id=1, source_target_pairs={{252,0},{0,4},{4,8},{8,12},{12,16},{16,20},{20,24},{24,28},{28,32}... | collective-permute-start | bytes 1179656 | tf_op jit(solution)/shard_map/while/body/eval_jaxpr/ppermute | solution.py:10
  136.5 12.4 %collective-permute-start.1 = (bf16[6,128,256]{2,1,0:T(8,128)(2,1)S(1)}, bf16[6,128,256]{2,1,0:T(8,128)(2,1)S(1)}, u32[]{:S(2)}, u32[]{:S(2)}) collective-permute-start(bf16[6,128,256]{2,1,0:T(8,128)(2,1)S(1)} %copy.61), channel_id=1, source_target_pairs={{252,0},{0,4},{4,8},{8,12},{12,16},{16,20},{20,24},{24,28},{28,32}... | collective-permute-start | bytes 1179656 | tf_op jit(solution)/shard_map/while/body/eval_jaxpr/ppermute | solution.py:10
  148.9 12.4 %collective-permute-start.1 = (bf16[6,128,256]{2,1,0:T(8,128)(2,1)S(1)}, bf16[6,128,256]{2,1,0:T(8,128)(2,1)S(1)}, u32[]{:S(2)}, u32[]{:S(2)}) collective-permute-start(bf16[6,128,256]{2,1,0:T(8,128)(2,1)S(1)} %copy.61), channel_id=1, source_target_pairs={{252,0},{0,4},{4,8},{8,12},{12,16},{16,20},{20,24},{24,28},{28,32}... | collective-permute-start | bytes 1179656 | tf_op jit(solution)/shard_map/while/body/eval_jaxpr/ppermute | solution.py:10
  161.4 12.4 %collective-permute-start.1 = (bf16[6,128,256]{2,1,0:T(8,128)(2,1)S(1)}, bf16[6,128,256]{2,1,0:T(8,128)(2,1)S(1)}, u32[]{:S(2)}, u32[]{:S(2)}) collective-permute-start(bf16[6,128,256]{2,1,0:T(8,128)(2,1)S(1)} %copy.61), channel_id=1, source_target_pairs={{252,0},{0,4},{4,8},{8,12},{12,16},{16,20},{20,24},{24,28},{28,32}... | collective-permute-start | bytes 1179656 | tf_op jit(solution)/shard_map/while/body/eval_jaxpr/ppermute | solution.py:10
  173.8 13.5 %collective-permute-start.1 = (bf16[6,128,256]{2,1,0:T(8,128)(2,1)S(1)}, bf16[6,128,256]{2,1,0:T(8,128)(2,1)S(1)}, u32[]{:S(2)}, u32[]{:S(2)}) collective-permute-start(bf16[6,128,256]{2,1,0:T(8,128)(2,1)S(1)} %copy.61), channel_id=1, source_target_pairs={{252,0},{0,4},{4,8},{8,12},{12,16},{16,20},{20,24},{24,28},{28,32}... | collective-permute-start | bytes 1179656 | tf_op jit(solution)/shard_map/while/body/eval_jaxpr/ppermute | solution.py:10
  187.4 14.6 %collective-permute-start.1 = (bf16[6,128,256]{2,1,0:T(8,128)(2,1)S(1)}, bf16[6,128,256]{2,1,0:T(8,128)(2,1)S(1)}, u32[]{:S(2)}, u32[]{:S(2)}) collective-permute-start(bf16[6,128,256]{2,1,0:T(8,128)(2,1)S(1)} %copy.61), channel_id=1, source_target_pairs={{252,0},{0,4},{4,8},{8,12},{12,16},{16,20},{20,24},{24,28},{28,32}... | collective-permute-start | bytes 1179656 | tf_op jit(solution)/shard_map/while/body/eval_jaxpr/ppermute | solution.py:10
  202.0 15.7 %collective-permute-start.1 = (bf16[6,128,256]{2,1,0:T(8,128)(2,1)S(1)}, bf16[6,128,256]{2,1,0:T(8,128)(2,1)S(1)}, u32[]{:S(2)}, u32[]{:S(2)}) collective-permute-start(bf16[6,128,256]{2,1,0:T(8,128)(2,1)S(1)} %copy.61), channel_id=1, source_target_pairs={{252,0},{0,4},{4,8},{8,12},{12,16},{16,20},{20,24},{24,28},{28,32}... | collective-permute-start | bytes 1179656 | tf_op jit(solution)/shard_map/while/body/eval_jaxpr/ppermute | solution.py:10
  217.7 16.7 %collective-permute-start.1 = (bf16[6,128,256]{2,1,0:T(8,128)(2,1)S(1)}, bf16[6,128,256]{2,1,0:T(8,128)(2,1)S(1)}, u32[]{:S(2)}, u32[]{:S(2)}) collective-permute-start(bf16[6,128,256]{2,1,0:T(8,128)(2,1)S(1)} %copy.61), channel_id=1, source_target_pairs={{252,0},{0,4},{4,8},{8,12},{12,16},{16,20},{20,24},{24,28},{28,32}... | collective-permute-start | bytes 1179656 | tf_op jit(solution)/shard_map/while/body/eval_jaxpr/ppermute | solution.py:10
  234.5 15.9 %collective-permute-start.1 = (bf16[6,128,256]{2,1,0:T(8,128)(2,1)S(1)}, bf16[6,128,256]{2,1,0:T(8,128)(2,1)S(1)}, u32[]{:S(2)}, u32[]{:S(2)}) collective-permute-start(bf16[6,128,256]{2,1,0:T(8,128)(2,1)S(1)} %copy.61), channel_id=1, source_target_pairs={{252,0},{0,4},{4,8},{8,12},{12,16},{16,20},{20,24},{24,28},{28,32}... | collective-permute-start | bytes 1179656 | tf_op jit(solution)/shard_map/while/body/eval_jaxpr/ppermute | solution.py:10
  250.4 15.0 %collective-permute-start.1 = (bf16[6,128,256]{2,1,0:T(8,128)(2,1)S(1)}, bf16[6,128,256]{2,1,0:T(8,128)(2,1)S(1)}, u32[]{:S(2)}, u32[]{:S(2)}) collective-permute-start(bf16[6,128,256]{2,1,0:T(8,128)(2,1)S(1)} %copy.61), channel_id=1, source_target_pairs={{252,0},{0,4},{4,8},{8,12},{12,16},{16,20},{20,24},{24,28},{28,32}... | collective-permute-start | bytes 1179656 | tf_op jit(solution)/shard_map/while/body/eval_jaxpr/ppermute | solution.py:10
  271.8 1.5 copy-start.6
  271.8 1.5 copy-start.4
  271.9 1.5 copy-start.1
  271.9 1.5 copy-start.2
  271.9 59.1 %copy-start.5 = (bf16[768,256]{1,0:T(8,128)(2,1)S(1)}, bf16[768,256]{1,0:T(8,128)(2,1)}, u32[]{:S(2)}) copy-start(bf16[768,256]{1,0:T(8,128)(2,1)} %param.18) | copy-start | bytes 1179652
  273.1 494.3 %reduce-scatter.2.cloned.1.call-start = ((), (), s32[]{:S(2)}) async-start(), calls=%async_computation.2 | async-start | bytes 491520 | tf_op jit(solution)/shard_map/reduce_scatter | solution.py:145
  333.8 0.7 copy-start.3
  342.1 24.4 %collective-permute-start = (f32[6,128,256]{2,1,0:T(8,128)}, f32[6,128,256]{2,1,0:T(8,128)S(1)}, u32[]{:S(2)}, u32[]{:S(2)}) collective-permute-start(f32[6,128,256]{2,1,0:T(8,128)} %copy.54), channel_id=1, source_target_pairs={{4,0},{8,4},{12,8},{16,12},{20,16},{24,20},{28,24},{32,28},{36,32}... | collective-permute-start | bytes 2359304 | tf_op jit(solution)/shard_map/while/body/eval_jaxpr/ppermute | solution.py:10
  369.8 24.0 %collective-permute-start = (f32[6,128,256]{2,1,0:T(8,128)}, f32[6,128,256]{2,1,0:T(8,128)S(1)}, u32[]{:S(2)}, u32[]{:S(2)}) collective-permute-start(f32[6,128,256]{2,1,0:T(8,128)} %copy.54), channel_id=1, source_target_pairs={{4,0},{8,4},{12,8},{16,12},{20,16},{24,20},{28,24},{32,28},{36,32}... | collective-permute-start | bytes 2359304 | tf_op jit(solution)/shard_map/while/body/eval_jaxpr/ppermute | solution.py:10
  397.1 23.1 %collective-permute-start = (f32[6,128,256]{2,1,0:T(8,128)}, f32[6,128,256]{2,1,0:T(8,128)S(1)}, u32[]{:S(2)}, u32[]{:S(2)}) collective-permute-start(f32[6,128,256]{2,1,0:T(8,128)} %copy.54), channel_id=1, source_target_pairs={{4,0},{8,4},{12,8},{16,12},{20,16},{24,20},{28,24},{32,28},{36,32}... | collective-permute-start | bytes 2359304 | tf_op jit(solution)/shard_map/while/body/eval_jaxpr/ppermute | solution.py:10
  423.4 22.2 %collective-permute-start = (f32[6,128,256]{2,1,0:T(8,128)}, f32[6,128,256]{2,1,0:T(8,128)S(1)}, u32[]{:S(2)}, u32[]{:S(2)}) collective-permute-start(f32[6,128,256]{2,1,0:T(8,128)} %copy.54), channel_id=1, source_target_pairs={{4,0},{8,4},{12,8},{16,12},{20,16},{24,20},{28,24},{32,28},{36,32}... | collective-permute-start | bytes 2359304 | tf_op jit(solution)/shard_map/while/body/eval_jaxpr/ppermute | solution.py:10
  448.8 21.2 %collective-permute-start = (f32[6,128,256]{2,1,0:T(8,128)}, f32[6,128,256]{2,1,0:T(8,128)S(1)}, u32[]{:S(2)}, u32[]{:S(2)}) collective-permute-start(f32[6,128,256]{2,1,0:T(8,128)} %copy.54), channel_id=1, source_target_pairs={{4,0},{8,4},{12,8},{16,12},{20,16},{24,20},{28,24},{32,28},{36,32}... | collective-permute-start | bytes 2359304 | tf_op jit(solution)/shard_map/while/body/eval_jaxpr/ppermute | solution.py:10
  473.3 20.3 %collective-permute-start = (f32[6,128,256]{2,1,0:T(8,128)}, f32[6,128,256]{2,1,0:T(8,128)S(1)}, u32[]{:S(2)}, u32[]{:S(2)}) collective-permute-start(f32[6,128,256]{2,1,0:T(8,128)} %copy.54), channel_id=1, source_target_pairs={{4,0},{8,4},{12,8},{16,12},{20,16},{24,20},{28,24},{32,28},{36,32}... | collective-permute-start | bytes 2359304 | tf_op jit(solution)/shard_map/while/body/eval_jaxpr/ppermute | solution.py:10
  496.9 19.4 %collective-permute-start = (f32[6,128,256]{2,1,0:T(8,128)}, f32[6,128,256]{2,1,0:T(8,128)S(1)}, u32[]{:S(2)}, u32[]{:S(2)}) collective-permute-start(f32[6,128,256]{2,1,0:T(8,128)} %copy.54), channel_id=1, source_target_pairs={{4,0},{8,4},{12,8},{16,12},{20,16},{24,20},{28,24},{32,28},{36,32}... | collective-permute-start | bytes 2359304 | tf_op jit(solution)/shard_map/while/body/eval_jaxpr/ppermute | solution.py:10
  519.5 18.5 %collective-permute-start = (f32[6,128,256]{2,1,0:T(8,128)}, f32[6,128,256]{2,1,0:T(8,128)S(1)}, u32[]{:S(2)}, u32[]{:S(2)}) collective-permute-start(f32[6,128,256]{2,1,0:T(8,128)} %copy.54), channel_id=1, source_target_pairs={{4,0},{8,4},{12,8},{16,12},{20,16},{24,20},{28,24},{32,28},{36,32}... | collective-permute-start | bytes 2359304 | tf_op jit(solution)/shard_map/while/body/eval_jaxpr/ppermute | solution.py:10
  541.3 17.6 %collective-permute-start = (f32[6,128,256]{2,1,0:T(8,128)}, f32[6,128,256]{2,1,0:T(8,128)S(1)}, u32[]{:S(2)}, u32[]{:S(2)}) collective-permute-start(f32[6,128,256]{2,1,0:T(8,128)} %copy.54), channel_id=1, source_target_pairs={{4,0},{8,4},{12,8},{16,12},{20,16},{24,20},{28,24},{32,28},{36,32}... | collective-permute-start | bytes 2359304 | tf_op jit(solution)/shard_map/while/body/eval_jaxpr/ppermute | solution.py:10
  562.1 17.1 %collective-permute-start = (f32[6,128,256]{2,1,0:T(8,128)}, f32[6,128,256]{2,1,0:T(8,128)S(1)}, u32[]{:S(2)}, u32[]{:S(2)}) collective-permute-start(f32[6,128,256]{2,1,0:T(8,128)} %copy.54), channel_id=1, source_target_pairs={{4,0},{8,4},{12,8},{16,12},{20,16},{24,20},{28,24},{32,28},{36,32}... | collective-permute-start | bytes 2359304 | tf_op jit(solution)/shard_map/while/body/eval_jaxpr/ppermute | solution.py:10
  582.4 16.8 %collective-permute-start = (f32[6,128,256]{2,1,0:T(8,128)}, f32[6,128,256]{2,1,0:T(8,128)S(1)}, u32[]{:S(2)}, u32[]{:S(2)}) collective-permute-start(f32[6,128,256]{2,1,0:T(8,128)} %copy.54), channel_id=1, source_target_pairs={{4,0},{8,4},{12,8},{16,12},{20,16},{24,20},{28,24},{32,28},{36,32}... | collective-permute-start | bytes 2359304 | tf_op jit(solution)/shard_map/while/body/eval_jaxpr/ppermute | solution.py:10
  602.4 16.8 %collective-permute-start = (f32[6,128,256]{2,1,0:T(8,128)}, f32[6,128,256]{2,1,0:T(8,128)S(1)}, u32[]{:S(2)}, u32[]{:S(2)}) collective-permute-start(f32[6,128,256]{2,1,0:T(8,128)} %copy.54), channel_id=1, source_target_pairs={{4,0},{8,4},{12,8},{16,12},{20,16},{24,20},{28,24},{32,28},{36,32}... | collective-permute-start | bytes 2359304 | tf_op jit(solution)/shard_map/while/body/eval_jaxpr/ppermute | solution.py:10
  622.4 16.8 %collective-permute-start = (f32[6,128,256]{2,1,0:T(8,128)}, f32[6,128,256]{2,1,0:T(8,128)S(1)}, u32[]{:S(2)}, u32[]{:S(2)}) collective-permute-start(f32[6,128,256]{2,1,0:T(8,128)} %copy.54), channel_id=1, source_target_pairs={{4,0},{8,4},{12,8},{16,12},{20,16},{24,20},{28,24},{32,28},{36,32}... | collective-permute-start | bytes 2359304 | tf_op jit(solution)/shard_map/while/body/eval_jaxpr/ppermute | solution.py:10
  642.5 17.4 %collective-permute-start = (f32[6,128,256]{2,1,0:T(8,128)}, f32[6,128,256]{2,1,0:T(8,128)S(1)}, u32[]{:S(2)}, u32[]{:S(2)}) collective-permute-start(f32[6,128,256]{2,1,0:T(8,128)} %copy.54), channel_id=1, source_target_pairs={{4,0},{8,4},{12,8},{16,12},{20,16},{24,20},{28,24},{32,28},{36,32}... | collective-permute-start | bytes 2359304 | tf_op jit(solution)/shard_map/while/body/eval_jaxpr/ppermute | solution.py:10
  663.1 28.8 %collective-permute-start = (f32[6,128,256]{2,1,0:T(8,128)}, f32[6,128,256]{2,1,0:T(8,128)S(1)}, u32[]{:S(2)}, u32[]{:S(2)}) collective-permute-start(f32[6,128,256]{2,1,0:T(8,128)} %copy.54), channel_id=1, source_target_pairs={{4,0},{8,4},{12,8},{16,12},{20,16},{24,20},{28,24},{32,28},{36,32}... | collective-permute-start | bytes 2359304 | tf_op jit(solution)/shard_map/while/body/eval_jaxpr/ppermute | solution.py:10
  694.2 20.5 %collective-permute-start.4 = (bf16[6,128,256]{2,1,0:T(8,128)(2,1)S(1)}, bf16[6,128,256]{2,1,0:T(8,128)(2,1)S(1)}, u32[]{:S(2)}, u32[]{:S(2)}) collective-permute-start(bf16[6,128,256]{2,1,0:T(8,128)(2,1)S(1)} %copy.33), channel_id=1, source_target_pairs={{64,0},{68,4},{72,8},{76,12},{80,16},{84,20},{88,24},{92,28},{96,3... | collective-permute-start | bytes 1179656 | tf_op jit(solution)/shard_map/ppermute | solution.py:10
  715.0 13.8 %collective-permute-start.5 = (bf16[6,128,256]{2,1,0:T(8,128)(2,1)S(1)}, bf16[6,128,256]{2,1,0:T(8,128)(2,1)S(1)}, u32[]{:S(2)}, u32[]{:S(2)}) collective-permute-start(bf16[6,128,256]{2,1,0:T(8,128)(2,1)S(1)} %broadcast_select_fusion), channel_id=1, source_target_pairs={{128,0},{132,4},{136,8},{140,12},{144,16},{148,20},{152,24},{156,2... | collective-permute-start | bytes 1179656 | tf_op jit(solution)/shard_map/ppermute | solution.py:10
Sparse Core Ops, SparseCore 0:
  273.2 57.7 all-reduce.1
  729.8 37.5 reduce-scatter.1
where the time goes:
time: 778 us; the launch traced here: 776 us
  waiting for transfers between devices  412 us (53%)
  starting transfers between devices  139 us (18%)
  matrix products  117 us (15%)
  local copies, waits for them, and re-layouts  65.6 us (8%)
  other arithmetic  25.3 us (3%)
  between operations  14.3 us (2%)
    ppermute x34, waiting for transfers between devices, passed_along(): return lax.ppermute(block, axis, route)  320 us
    ppermute x34, starting transfers between devices, passed_along(): return lax.ppermute(block, axis, route)  139 us
    dot_general x32, matrix products, padded_blocks(): jnp.einsum('rk,kif->rif', placement, product, precision=lax.Precision.HIG...  65.9 us
    psum x1, waiting for transfers between devices, on_device(): summed = lax.psum(partial_agg, 'rep')  57.4 us
    dot_general x32, matrix products, padded_blocks(): jnp.einsum(pattern, weights, picked, preferred_element_type=jnp.float32)  47.1 us
    reduce_scatter x1, waiting for transfers between devices, on_device(): lax.psum_scatter(returned.reshape(panel_rows, feature_width).astype(jnp.b...  34.9 us
    lt x31, other arithmetic, padded_blocks(): slot_ids < count_here  20.2 us
    gather x32, local copies, waits for them, and re-layouts, padded_blocks(): picked = jnp.take(source3, source_ids, axis=0)  19.1 us
  transfers between devices with their start and end apart: 36, of which 36 were waited for; matrix products, arithmetic and copies ran while one was open for 18% of the time, Pallas kernels for 0%

commit v1 on v0

v1 whole, which is shorter than its diff:
```python
import jax
import jax.numpy as jnp
from jax import lax
from jax.experimental import pallas as pl
from jax.experimental.pallas import tpu as pltpu
from jax.sharding import PartitionSpec as P

MESH = pl.DeviceIdType.MESH
F32 = jnp.float32
BF16 = jnp.bfloat16
NB = 6
BLK = 128
SLOTS = 12
PR = NB * BLK
HALF = PR // 2
HID = 256
QR = PR // 4


class Copies:
    def __init__(self, send_sems, recv_sems):
        self.send_sems, self.recv_sems = send_sems, recv_sems
        self.sends = 0
        self.recvs = 0
        self.pending = []

    def recv_slot(self):
        self.recvs += 1
        return self.recvs - 1

    def start(self, src, dst, recv_slot, device, cond=None, send_slot=None, track=True):
        if send_slot is None:
            send_slot = self.sends
            self.sends += 1
        copy = pltpu.make_async_remote_copy(
            src_ref=src,
            dst_ref=dst,
            send_sem=self.send_sems.at[send_slot],
            recv_sem=self.recv_sems.at[recv_slot],
            device_id=device,
            device_id_type=MESH,
        )
        if cond is None:
            copy.start()
        else:
            pl.when(cond)(lambda: copy.start())
        if track:
            self.pending.append((cond, copy))
        return send_slot

    def wait_recv(self, ref, recv_slot):
        pltpu.make_async_copy(ref, ref, self.recv_sems.at[recv_slot]).wait()

    def drain(self):
        for cond, copy in self.pending:
            if cond is None:
                copy.wait_send()
            else:
                pl.when(cond)(lambda copy=copy: copy.wait_send())
        self.pending = []


def kernel(
    rows_s, cols_s, cnt_s, feat, deg, cot_hbm, wself, wneigh, bias, w_hbm,
    out, grad,
    wv, wt, xbuf, zbuf, acc, lhs, rhs, stage, sstage, cot,
    mid_src, mid_in, sbuf, base,
    pbuf, opp_in, dir_in, znear, zfar, zone, chain_in, chain_out, fin_in,
    send_sems, recv_sems, load_sems, go_sem,
):
    i = lax.axis_index("rows")
    r = lax.axis_index("rep")
    z, yh, x, w = i // 8, lax.rem(i // 4, 2), lax.rem(i, 4), lax.rem(i, 8)
    lo, core = r // 2, lax.rem(r, 2)
    role = lax.rem(core + lo, 2)
    step = 1 - 2 * lo
    znext, zprev = lax.rem(z + step + 8, 8), lax.rem(z - step + 8, 8)
    xr, xl, xo = lax.rem(x + 1, 4), lax.rem(x + 3, 4), lax.rem(x + 2, 4)
    inner = jnp.logical_or(x == 1, x == 2)
    near_role, far_role = role == 0, role == 1

    def dev(z_, yh_, x_, lo_, role_):
        return (z_ * 8 + yh_ * 4 + x_, 2 * lo_ + lax.rem(role_ + lo_, 2))

    left, right = dev(z, yh, xl, lo, role), dev(z, yh, xr, lo, role)
    ahead, behind = dev(znext, yh, x, lo, role), dev(zprev, yh, x, lo, role)
    mate = dev(z, yh, x, lo, 1 - role)
    across = dev(z, 1 - yh, x, 1 - lo, role)

    def near(wp, w_at):
        return lax.rem(jnp.where(wp <= w_at, 1, 0) + lo, 2)

    load_w = pltpu.make_async_copy(w_hbm.at[0], wv, load_sems.at[0])
    load_w.start()
    load_cot = pltpu.make_async_copy(cot_hbm.at[pl.ds(r * QR, QR)], cot, load_sems.at[1])
    load_cot.start()

    barrier = pltpu.get_barrier_semaphore()
    partners = [left, right, ahead, behind]
    for other in range(1, 8):
        at = lax.rem(yh * 4 + r + other, 8)
        partners.append((z * 8 + (at // 4) * 4 + x, lax.rem(at, 4)))
    for partner in partners:
        pl.semaphore_signal(barrier, inc=1, device_id=partner, device_id_type=MESH)
    pl.semaphore_wait(barrier, len(partners))

    net = Copies(send_sems, recv_sems)
    order = (yh, 1 - yh)

    r_z0 = [net.recv_slot() for _ in order]
    r_z1 = [net.recv_slot() for _ in order]
    r_z2 = [net.recv_slot() for _ in order]
    r_dir = [[[net.recv_slot() for _ in range(2)] for _ in order] for _ in range(2)]
    r_opp = [[[net.recv_slot() for _ in range(2)] for _ in order] for _ in range(2)]

    def comp_direct(o, hh, idx, slots):
        for side, (nx, target) in enumerate(((xr, right), (xl, left))):
            flag = near(4 * hh + x, 4 * yh + nx)
            cond = flag == (1 if idx == 0 else 0)
            slots[side] = net.start(
                zbuf.at[idx, hh], xbuf.at[0, hh, x], r_dir[0][o][side], target,
                cond=cond, send_slot=slots[side], track=True,
            )

    @pl.when(near_role)
    def _():
        zbuf[0, yh] = feat[...]

    net.start(feat, zbuf.at[0, yh], r_z0[1], across, cond=near_role)
    comp_slots = [[None, None], [None, None]]
    for o, hh in enumerate(order):
        if o == 0:
            @pl.when(far_role)
            def _(o=o, hh=hh):
                net.wait_recv(zbuf.at[0, hh], r_z0[o])
        else:
            net.wait_recv(zbuf.at[0, hh], r_z0[o])
        net.start(zbuf.at[0, hh], xbuf.at[1, hh, x], r_z1[o], ahead)
        comp_direct(o, hh, 0, comp_slots[o])

    for o, hh in enumerate(order):
        net.wait_recv(xbuf.at[1, hh, x], r_z1[o])
        net.start(xbuf.at[1, hh, x], zbuf.at[1, hh], r_z2[o], ahead)
        net.start(xbuf.at[1, hh, x], xbuf.at[1, hh, x], r_dir[1][o][0], right)
        net.start(xbuf.at[1, hh, x], xbuf.at[1, hh, x], r_dir[1][o][1], left)

    load_w.wait()
    acc[...] = jnp.zeros_like(acc)

    def block_of(cl, hh, xs):
        wp = 4 * hh + xs
        if cl == 1:
            return 8 + w - wp
        return lax.rem(w - wp + 16, 16)

    def fill(j, blocks, src, source_ids, target_ids, transpose):
        count = cnt_s[0, j]
        for k in range(SLOTS):
            rhs[pl.ds(k * BLK, BLK), :] = src[source_ids[0, j, k]]
        for k in range(SLOTS):
            a = blocks[j, k]
            if transpose:
                wt[j, k] = a.T
            target = jnp.where(k < count, target_ids[0, j, k], -1)
            for b in range(NB):
                lhs[pl.ds(b * BLK, BLK), pl.ds(k * BLK, BLK)] = jnp.where(
                    target == b, a, jnp.zeros_like(a)
                )

    def forward(cl, xs_list):
        def body(t, carry):
            hh = lax.rem(t, 2)
            xs = xs_list[0]
            for n in range(1, len(xs_list)):
                xs = jnp.where(t // 2 == n, xs_list[n], xs)
            for b in range(NB):
                stage[b] = xbuf[cl, hh, xs, pl.ds(b * BLK, BLK), :]
            fill(block_of(cl, hh, xs), wv, stage, cols_s, rows_s, True)
            acc[...] += jnp.dot(lhs[...], rhs[...], preferred_element_type=F32)
            return carry

        lax.fori_loop(0, 2 * len(xs_list), body, 0)

    forward(1, [x])

    def pass_opposite(cl, o, hh):
        if cl == 0 and o == 0:
            net.wait_recv(xbuf.at[cl, hh, xl], r_dir[cl][o][0])
            net.start(xbuf.at[cl, hh, xl], xbuf.at[cl, hh, xl], r_opp[cl][o][0], right, cond=inner)
            net.wait_recv(xbuf.at[cl, hh, xr], r_dir[cl][o][1])
            net.start(xbuf.at[cl, hh, xr], xbuf.at[cl, hh, xr], r_opp[cl][o][0], left, cond=inner)
        else:
            a, b = pl.ds(0, HALF), pl.ds(HALF, HALF)
            net.wait_recv(xbuf.at[cl, hh, xl], r_dir[cl][o][0])
            net.start(xbuf.at[cl, hh, xl, a], xbuf.at[cl, hh, xl, a], r_opp[cl][o][0], right)
            net.wait_recv(xbuf.at[cl, hh, xr], r_dir[cl][o][1])
            net.start(xbuf.at[cl, hh, xr, b], xbuf.at[cl, hh, xr, b], r_opp[cl][o][1], left)

    def wait_opposite(cl, o, hh):
        if cl == 0 and o == 0:
            net.wait_recv(xbuf.at[cl, hh, xo], r_opp[cl][o][0])
        else:
            net.wait_recv(xbuf.at[cl, hh, xo, pl.ds(0, HALF)], r_opp[cl][o][0])
            net.wait_recv(xbuf.at[cl, hh, xo, pl.ds(HALF, HALF)], r_opp[cl][o][1])

    for o, hh in enumerate(order):
        pass_opposite(1, o, hh)
        net.wait_recv(zbuf.at[1, hh], r_z2[o])
        net.start(zbuf.at[1, hh], zbuf.at[0, hh], r_z0[o], mate, cond=near_role)
        comp_direct(o, hh, 1, comp_slots[o])
        own = near(4 * hh + x, w)
        xbuf[0, hh, x] = zbuf[1 - own, hh]

    forward(1, [xl, xr])
    for o, hh in enumerate(order):
        pass_opposite(0, o, hh)
    for o, hh in enumerate(order):
        wait_opposite(1, o, hh)
    forward(1, [xo])
    forward(0, [x, xl, xr])
    for o, hh in enumerate(order):
        wait_opposite(0, o, hh)
    forward(0, [xo])

    mid_src[...] = acc[...].astype(BF16)
    r_mid, r_sc = net.recvs, net.recvs + 4
    net.recvs += 8
    peers = [lax.rem(r + n, 4) for n in range(1, 4)]
    for peer in peers:
        net.start(
            mid_src.at[pl.ds(pl.multiple_of(peer * QR, QR), QR)], mid_in.at[r], r_mid + r, (i, peer)
        )
    own_rows = pl.ds(pl.multiple_of(r * QR, QR), QR)
    total = acc[own_rows, :]
    f_own = feat[own_rows, :]
    divisor = deg[...]
    divisor = jnp.concatenate([divisor, divisor], axis=1)
    preact = jnp.dot(f_own, wself[...], preferred_element_type=F32) + bias[...]
    load_cot.wait()
    for peer in peers:
        net.wait_recv(mid_in.at[peer], r_mid + peer)
        total = total + mid_in[peer].astype(F32)
    neighbours = (total / divisor).astype(BF16)
    preact = preact + jnp.dot(neighbours, wneigh[...], preferred_element_type=F32)
    sig = jax.nn.sigmoid(preact)
    slope = sig * (1.0 + preact * (1.0 - sig))
    pre_grad = (cot[...].astype(F32) * slope).astype(BF16)
    contract = (((1,), (1,)), ((), ()))
    scaled = lax.dot_general(pre_grad, wneigh[...], contract, preferred_element_type=F32)
    sbuf[own_rows, :] = (scaled / divisor).astype(BF16)
    for peer in peers:
        net.start(sbuf.at[own_rows], sbuf.at[own_rows], r_sc + r, (i, peer))
    out[...] = (preact * sig).astype(BF16)
    base[...] = lax.dot_general(pre_grad, wself[...], contract, preferred_element_type=F32)
    for peer in peers:
        net.wait_recv(sbuf.at[pl.ds(pl.multiple_of(peer * QR, QR), QR)], r_sc + peer)
    for b in range(NB):
        sstage[b] = sbuf[pl.ds(b * BLK, BLK), :]

    b_opp = [[net.recvs + 4 * cl + 2 * o for o in range(2)] for cl in range(2)]
    net.recvs += 8
    b_dir = [[[net.recv_slot() for _ in range(2)] for _ in order] for _ in range(2)]
    b_chain = [[net.recv_slot() for _ in order] for _ in range(3)]

    def backward(cl, xs_list):
        def body(t, carry):
            hh = lax.rem(t, 2)
            xs = xs_list[0]
            for n in range(1, len(xs_list)):
                xs = jnp.where(t // 2 == n, xs_list[n], xs)
            fill(block_of(cl, hh, xs), wt, sstage, rows_s, cols_s, False)
            pbuf[cl, hh, xs] = jnp.dot(lhs[...], rhs[...], preferred_element_type=F32).astype(BF16)
            return carry

        lax.fori_loop(0, 2 * len(xs_list), body, 0)

    low, high = pl.ds(0, HALF), pl.ds(HALF, HALF)

    def send_opposite(cl):
        for o, hh in enumerate(order):
            if cl == 0 and o == 0:
                side = jnp.where(x <= 1, 0, 1)
                target = dev(z, yh, jnp.where(x <= 1, xr, xl), lo, role)
                net.start(pbuf.at[cl, hh, xo], opp_in.at[cl, o, side], b_opp[cl][o] + side, target)
            else:
                net.start(pbuf.at[cl, hh, xo, low], opp_in.at[cl, o, 1, low], b_opp[cl][o] + 1, left)
                net.start(pbuf.at[cl, hh, xo, high], opp_in.at[cl, o, 0, high], b_opp[cl][o], right)

    def send_direct(cl):
        for o, hh in enumerate(order):
            def merge(side, xs, part, o=o, hh=hh):
                net.wait_recv(opp_in.at[cl, o, side, part], b_opp[cl][o] + side)
                pbuf[cl, hh, xs, part, :] = (
                    pbuf[cl, hh, xs, part, :].astype(F32) + opp_in[cl, o, side, part, :].astype(F32)
                ).astype(BF16)

            if cl == 0 and o == 0:
                @pl.when(inner)
                def _(merge=merge):
                    merge(0, xr, pl.ds(0, PR))
                    merge(1, xl, pl.ds(0, PR))
            else:
                merge(0, xr, high)
                merge(1, xl, low)
            net.start(pbuf.at[cl, hh, xl], dir_in.at[cl, o, 1], b_dir[cl][o][1], left)
            net.start(pbuf.at[cl, hh, xr], dir_in.at[cl, o, 0], b_dir[cl][o][0], right)

    backward(0, [xo, xl, xr])

    @pl.when(near_role)
    def _():
        pl.semaphore_wait(go_sem, 1)

    send_opposite(0)
    backward(1, [xo])
    send_direct(0)
    send_opposite(1)
    backward(1, [xl, xr])
    send_direct(1)

    @pl.when(far_role)
    def _():
        pl.semaphore_signal(go_sem, inc=1, device_id=mate, device_id_type=MESH)

    backward(0, [x])
    for o, hh in enumerate(order):
        net.wait_recv(dir_in.at[0, o, 0], b_dir[0][o][0])
        net.wait_recv(dir_in.at[0, o, 1], b_dir[0][o][1])
        wp = 4 * hh + x
        n_own = near(wp, w).astype(F32)
        n_left = near(wp, 4 * yh + xl).astype(F32)
        n_right = near(wp, 4 * yh + xr).astype(F32)
        v_own = pbuf[0, hh, x].astype(F32)
        v_left = dir_in[0, o, 0].astype(F32)
        v_right = dir_in[0, o, 1].astype(F32)
        znear[o] = n_own * v_own + n_left * v_left + n_right * v_right
        far = (1.0 - n_own) * v_own + (1.0 - n_left) * v_left + (1.0 - n_right) * v_right
        zfar[o] = far

        @pl.when(far_role)
        def _(o=o, far=far):
            chain_out[2, o] = far.astype(BF16)

        net.start(chain_out.at[2, o], chain_in.at[1, o], b_chain[1][o], behind, cond=far_role)
    backward(1, [x])
    for o, hh in enumerate(order):
        net.wait_recv(dir_in.at[1, o, 0], b_dir[1][o][0])
        net.wait_recv(dir_in.at[1, o, 1], b_dir[1][o][1])
        zone[o] = (
            pbuf[1, hh, x].astype(F32) + dir_in[1, o, 0].astype(F32) + dir_in[1, o, 1].astype(F32)
        )
    for o in range(2):
        @pl.when(near_role)
        def _(o=o):
            net.wait_recv(chain_in.at[2, o], b_chain[2][o])
            chain_out[2, o] = (zfar[o] + chain_in[2, o].astype(F32)).astype(BF16)

        net.start(chain_out.at[2, o], chain_in.at[1, o], b_chain[1][o], behind, cond=near_role)
    for o in range(2):
        net.wait_recv(chain_in.at[1, o], b_chain[1][o])
        chain_out[1, o] = (zone[o] + chain_in[1, o].astype(F32)).astype(BF16)
        net.start(chain_out.at[1, o], chain_in.at[0, o], b_chain[0][o], behind)
    r_fin = net.recvs
    net.recvs += 4
    mine = 2 * lo + yh
    for o, hh in enumerate(order):
        net.wait_recv(chain_in.at[0, o], b_chain[0][o])
        chain_out[0, o] = (znear[o] + chain_in[0, o].astype(F32)).astype(BF16)
        net.start(chain_out.at[0, o], chain_in.at[2, o], b_chain[2][o], mate, cond=far_role)
        for quarter in range(4):
            rows = pl.ds(quarter * QR, QR)
            if o == 0:
                away = jnp.logical_and(near_role, r != quarter)

                @pl.when(jnp.logical_and(near_role, r == quarter))
                def _(rows=rows, o=o):
                    fin_in[mine] = chain_out[0, o, rows, :]
            else:
                away = near_role
            net.start(
                chain_out.at[0, o, rows], fin_in.at[mine], r_fin + mine, (z * 8 + hh * 4 + x, quarter),
                cond=away,
            )
    result = base[...]
    for source in range(4):
        @pl.when(jnp.logical_or(far_role, mine != source))
        def _(source=source):
            net.wait_recv(fin_in.at[source], r_fin + source)

    for source in range(4):
        result = result + fin_in[source].astype(F32)
    grad[...] = result.astype(BF16)
    net.drain()


def on_device(
    features, degrees, cotangent, self_weight, neigh_weight, bias_vector,
    block_values, block_rows, block_cols, block_count,
):
    r = lax.axis_index("rep")
    deg = lax.dynamic_slice_in_dim(degrees, r * QR, QR, 0).astype(F32)
    deg = jnp.broadcast_to(deg[:, None], (QR, BLK))
    vmem = pl.BlockSpec(memory_space=pltpu.VMEM)
    smem = pl.BlockSpec(memory_space=pltpu.SMEM)
    anyspace = pl.BlockSpec(memory_space=pl.ANY)
    panel = (PR, HID)
    return pl.pallas_call(
        kernel,
        out_shape=(
            jax.ShapeDtypeStruct((QR, HID), BF16),
            jax.ShapeDtypeStruct((QR, HID), BF16),
        ),
        in_specs=[smem, smem, smem, vmem, vmem, anyspace, vmem, vmem, vmem, anyspace],
        out_specs=(vmem, vmem),
        scratch_shapes=[
            pltpu.VMEM((16, SLOTS, BLK, BLK), BF16),
            pltpu.VMEM((16, SLOTS, BLK, BLK), BF16),
            pltpu.VMEM((2, 2, 4) + panel, BF16),
            pltpu.VMEM((2, 2) + panel, BF16),
            pltpu.VMEM(panel, F32),
            pltpu.VMEM((PR, SLOTS * BLK), BF16),
            pltpu.VMEM((SLOTS * BLK, HID), BF16),
            pltpu.VMEM((NB, BLK, HID), BF16),
            pltpu.VMEM((NB, BLK, HID), BF16),
            pltpu.VMEM((QR, HID), BF16),
            pltpu.VMEM(panel, BF16),
            pltpu.VMEM((4, QR, HID), BF16),
            pltpu.VMEM(panel, BF16),
            pltpu.VMEM((QR, HID), F32),
            pltpu.VMEM((2, 2, 4) + panel, BF16),
            pltpu.VMEM((2, 2, 2) + panel, BF16),
            pltpu.VMEM((2, 2, 2) + panel, BF16),
            pltpu.VMEM((2,) + panel, F32),
            pltpu.VMEM((2,) + panel, F32),
            pltpu.VMEM((2,) + panel, F32),
            pltpu.VMEM((3, 2) + panel, BF16),
            pltpu.VMEM((3, 2) + panel, BF16),
            pltpu.VMEM((4, QR, HID), BF16),
            pltpu.SemaphoreType.DMA((96,)),
            pltpu.SemaphoreType.DMA((96,)),
            pltpu.SemaphoreType.DMA((2,)),
            pltpu.SemaphoreType.REGULAR,
        ],
        compiler_params=pltpu.CompilerParams(
            collective_id=0, has_side_effects=True, vmem_limit_bytes=60 * 1024 * 1024
        ),
        name="sage_layer",
    )(
        block_rows, block_cols, block_count, features, deg, cotangent,
        self_weight, neigh_weight, bias_vector.astype(F32)[None, :], block_values,
    )


def solution(mesh):
    return jax.shard_map(
        on_device,
        mesh=mesh,
        in_specs=(
            P("rows", None),
            P("rows"),
            P("rows", None),
            P(),
            P(),
            P(),
            P("rows", "rep", None, None, None),
            P("rows", "rep", None),
            P("rows", "rep", None),
            P("rows", "rep"),
        ),
        out_specs=(P(("rows", "rep"), None), P(("rows", "rep"), None)),
        check_vma=False,
    )
```

time: 778 us -> 186 us (0.24)
  waiting for transfers between devices: 412 us -> 0 us
  Pallas kernels: 0 us -> 176 us
  starting transfers between devices: 139 us -> 0 us
  matrix products: 117 us -> 0 us
  local copies, waits for them, and re-layouts: 65.6 us -> 6.53 us
  other arithmetic: 25.3 us -> 1.96 us
  between operations: 14.3 us -> 0.64 us
    ppermute x34 -> x0, waiting for transfers between devices: 320 us -> none  [passed_along(): return lax.ppermute(block, axis, route)]
    pallas_call x0 -> x1, Pallas kernels: none -> 176 us  [on_device(): pl.pallas_call(kernel, out_shape=(jax.ShapeDtypeStruct((QR, HID), BF16),...]
    ppermute x34 -> x0, starting transfers between devices: 139 us -> none  [passed_along(): return lax.ppermute(block, axis, route)]
    dot_general x68 -> x0, matrix products: 117 us -> none  [the longest x32 65.9 us: padded_blocks(): jnp.einsum('rk,kif->rif', placement, product, precision=lax.Precision.HIG...]
    psum x1 -> x0, waiting for transfers between devices: 57.4 us -> none  [on_device(): summed = lax.psum(partial_agg, 'rep')]
    reduce_scatter x1 -> x0, waiting for transfers between devices: 34.9 us -> none  [on_device(): lax.psum_scatter(returned.reshape(panel_rows, feature_width).astype(jnp.b...]
    lt x31 -> x0, other arithmetic: 20.2 us -> none  [padded_blocks(): slot_ids < count_here]
    gather x32 -> x0, local copies, waits for them, and re-layouts: 19.1 us -> none  [padded_blocks(): picked = jnp.take(source3, source_ids, axis=0)]
  transfers between devices with their start and end apart: 36 -> 0, of which waited for: 36 -> 0; matrix products, arithmetic and copies ran while one was open for 18% -> 0% of each run, Pallas kernels for 0% -> 0%
where the time goes in v1:
time: 186 us
  Pallas kernels  176 us (95%)
  local copies, waits for them, and re-layouts  6.53 us (4%)
  other arithmetic  1.96 us (1%)
    pallas_call x1, Pallas kernels, on_device(): pl.pallas_call(kernel, out_shape=(jax.ShapeDtypeStruct((QR, HID), BF16),...  176 us
    unnamed x4, local copies, waits for them, and re-layouts  5.8 us

profile of v1, /device:TPU:1, one launch (start us, length us, event | category | flops | bytes accessed | tf_op | source)
XLA Modules:
  0.0 185.6 jit_solution(2347714143687709543)
XLA Ops:
  0.6 0.8 dynamic-slice_convert_fusion
  1.4 1.2 broadcast_in_dim.14
  2.6 1.4 copy.12.rows_s
  4.0 1.4 copy.13.cols_s
  5.3 0.7 broadcast_in_dim.11.deg
  6.0 176.5 %sage_layer.1 = (bf16[192,256]{1,0:T(8,128)(2,1)}, bf16[192,256]{1,0:T(8,128)(2,1)}) custom-call(s32[1,16,12]{2,1,0:T(8,128)} %copy.12.rows_s, s32[1,16,12]{2,1,0:T(8,128)} %copy.13.cols_s, s32[1,16]{1,0:T(1,128)} %cnt_s.1, bf16[768,256]{1,0:T(8,128)(2,1)} %feat.1, f32[192,128]{1,0:T(8,128)} %broadcast_in_dim.11.deg, bf16[768,256]{1,0:T(8,128)(2,1)} %cot_hbm.1, ...), custom_call_target="tpu_custom_call" | custom-call | tf_op jit(solution)/shard_map/sage_layer/pallas_call | solution.py:407
  182.5 1.5 copy.16
  184.1 1.5 copy.17

commit v2 on v1

v2 whole, which is shorter than its diff:
```python
import jax
import jax.numpy as jnp
from jax import lax
from jax.experimental import pallas as pl
from jax.experimental.pallas import tpu as pltpu
from jax.sharding import PartitionSpec as P

MESH = pl.DeviceIdType.MESH
F32 = jnp.float32
BF16 = jnp.bfloat16
NB = 6
BLK = 128
SLOTS = 12
PR = NB * BLK
HID = 256
QR = PR // 4
RB = 80
AR = PR - 4 * RB
HA = AR // 2
FWD_STEPS = 46
BWD_STEPS = 46
BWD_LATE = 10


def quarter_parts(start, size):
    parts = []
    for quarter in range(4):
        a, b = max(start, quarter * QR), min(start + size, (quarter + 1) * QR)
        if a < b:
            parts.append((a - start, b - a, quarter, a - quarter * QR))
    return parts


A_PARTS = quarter_parts(0, AR)
B_PARTS = [quarter_parts(AR + q * RB, RB) for q in range(4)]


def kernel(
    rows_s, cols_s, cnt_s, feat, deg, cot_hbm, wself, wneigh, bias, w_hbm,
    out, grad,
    wv, wt, xbuf, zbuf, acc, lhs, rhs, stage, sstage, cot, dcol,
    mid_src, mid_in, sbuf, base, rbuf,
    pbuf, opp_in, dir_in, znear, zfar, zone, chain_in, chain_out, fin_a,
    rin, tin, tout, tacc, fin_b,
    send_sems, recv_sems, load_sems, go_sem,
    s_rz, r_rz, s_src, s_y, r_y, s_p, r_p, s_t, r_t, s_fb, r_fb,
):
    i = lax.axis_index("rows")
    r = lax.axis_index("rep")
    z, yh, x, w = i // 8, lax.rem(i // 4, 2), lax.rem(i, 4), lax.rem(i, 8)
    lo, core = r // 2, lax.rem(r, 2)
    role = lax.rem(core + lo, 2)
    step = 1 - 2 * lo
    znext, zprev = lax.rem(z + step + 8, 8), lax.rem(z - step + 8, 8)
    xr, xl, xo = lax.rem(x + 1, 4), lax.rem(x + 3, 4), lax.rem(x + 2, 4)
    inner = jnp.logical_or(x == 1, x == 2)
    near_role, far_role = role == 0, role == 1
    relay = 2 * yh + role
    share = pl.ds(pl.multiple_of(AR + RB * relay, 16), RB)
    share_across = pl.ds(pl.multiple_of(AR + RB * (2 * (1 - yh) + role), 16), RB)

    def dev(z_, yh_, x_, lo_, role_):
        return (z_ * 8 + yh_ * 4 + x_, 2 * lo_ + lax.rem(role_ + lo_, 2))

    left, right = dev(z, yh, xl, lo, role), dev(z, yh, xr, lo, role)
    opposite = dev(z, yh, xo, lo, role)
    ahead, behind = dev(znext, yh, x, lo, role), dev(zprev, yh, x, lo, role)
    mate = dev(z, yh, x, lo, 1 - role)
    across = dev(z, 1 - yh, x, 1 - lo, role)

    def near(wp, w_at, lo_at=lo):
        return lax.rem(jnp.where(wp <= w_at, 1, 0) + lo_at, 2)

    load_w = pltpu.make_async_copy(w_hbm.at[0], wv, load_sems.at[0])
    load_w.start()
    load_cot = pltpu.make_async_copy(cot_hbm.at[pl.ds(r * QR, QR)], cot, load_sems.at[1])
    load_cot.start()

    barrier = pltpu.get_barrier_semaphore()

    def greet(n, carry):
        at = lax.rem(w * 4 + r + n, 32)
        pl.semaphore_signal(
            barrier, inc=1, device_id=(z * 8 + at // 4, lax.rem(at, 4)), device_id_type=MESH
        )
        return carry

    lax.fori_loop(1, 32, greet, 0)
    pl.semaphore_signal(barrier, inc=1, device_id=ahead, device_id_type=MESH)
    pl.semaphore_signal(barrier, inc=1, device_id=behind, device_id_type=MESH)
    pl.semaphore_wait(barrier, 33)

    sends, recvs, pending = [0], [0], []

    def recv_slot(n=1):
        recvs[0] += n
        return recvs[0] - n

    def copy_to(src, dst, send_sem, recv_sem, device):
        return pltpu.make_async_remote_copy(
            src_ref=src, dst_ref=dst, send_sem=send_sem, recv_sem=recv_sem,
            device_id=device, device_id_type=MESH,
        )

    def joined(cond, role_cond):
        if cond is None or role_cond is None:
            return role_cond if cond is None else cond
        return jnp.logical_and(cond, role_cond)

    def start(src, dst, slot, device, cond=None, role_cond=None, send_slot=None):
        if send_slot is None:
            send_slot = sends[0]
            sends[0] += 1
        copy = copy_to(src, dst, send_sems.at[send_slot], recv_sems.at[slot], device)
        both = joined(cond, role_cond)
        if both is None:
            copy.start()
        else:
            pl.when(both)(lambda: copy.start())
        pending.append((cond, role_cond, src.shape[-2], send_slot))
        return send_slot

    def wait_bytes(ref, sem):
        pltpu.make_async_copy(ref, ref, sem).wait()

    def wait_recv(ref, slot):
        wait_bytes(ref, recv_sems.at[slot])

    def drain():
        for cond, role_cond, rows, slot in pending:
            cond = joined(cond, role_cond)

            def wait(rows=rows, slot=slot):
                wait_bytes(zbuf.at[0, 0, pl.ds(0, rows)], send_sems.at[slot])

            if cond is None:
                wait()
            else:
                pl.when(cond)(wait)
        pending.clear()

    def drain_many(sems, count, rows):
        def wait(n, carry):
            wait_bytes(zbuf.at[0, 0, pl.ds(0, rows)], sems.at[n])
            return carry

        lax.fori_loop(0, count, wait, 0)

    order = (yh, 1 - yh)
    arows = pl.ds(0, AR)
    low, high = pl.ds(0, HA), pl.ds(HA, HA)

    not_quarter = [r != quarter for quarter in range(4)]
    near_side = [
        [near(4 * hh + x, 4 * yh + nx) == 1 for nx in (xr, xl)] for hh in order
    ]
    far_side = [
        [near(4 * hh + x, 4 * yh + nx) == 0 for nx in (xr, xl)] for hh in order
    ]

    r_z0 = [recv_slot() for _ in order]
    r_z1 = [recv_slot() for _ in order]
    r_z2 = [recv_slot() for _ in order]
    r_dir = [[[recv_slot() for _ in range(2)] for _ in order] for _ in range(2)]
    r_opp = [[[recv_slot() for _ in range(2)] for _ in order] for _ in range(2)]
    comp_slots = [[None, None], [None, None]]

    def comp_direct(o, hh, idx, src, role_cond=None):
        flags = near_side if idx == 0 else far_side
        for side, target in enumerate((right, left)):
            comp_slots[o][side] = start(
                src, xbuf.at[0, hh, x, arows], r_dir[0][o][side], target,
                cond=flags[o][side], role_cond=role_cond, send_slot=comp_slots[o][side],
            )

    own_a = feat.at[arows]
    start(own_a, xbuf.at[1, yh, x, arows], r_z1[0], ahead, role_cond=near_role)
    start(own_a, zbuf.at[0, yh], r_z0[1], across, role_cond=near_role)
    own_b = feat.at[share]
    copy_to(own_b, rbuf.at[1, yh, x], s_rz.at[0], r_rz.at[8], behind).start()
    copy_to(feat.at[share_across], rbuf.at[0, yh, x], s_src.at[0], r_rz.at[1], across).start()
    for n, (target, at) in enumerate(((right, 2), (left, 3), (opposite, 4))):
        copy_to(own_b, rbuf.at[0, yh, x], s_src.at[1 + n], r_rz.at[at], target).start()
    comp_direct(0, yh, 0, own_a, near_role)

    @pl.when(near_role)
    def _():
        zbuf[0, yh] = feat[arows, :]

    rbuf[0, yh, x] = feat[share, :]

    dcol_rows = deg[...].astype(F32)
    dcol_t = jnp.concatenate([dcol_rows, dcol_rows[0:2]], axis=0).T
    for b in range(NB):
        dcol[pl.ds(b * BLK, BLK), :] = jnp.broadcast_to(dcol_t[:, b : b + 1], (BLK, HID))

    acc[...] = jnp.zeros_like(acc)
    load_w.wait()

    def block_of(cl, wp):
        return jnp.where(cl == 1, 8 + w - wp, lax.rem(w - wp + 16, 16))

    def fill(j, blocks, src, source_ids, target_ids, transpose):
        count = cnt_s[0, j]
        for k in range(SLOTS):
            rhs[pl.ds(k * BLK, BLK), :] = src[source_ids[k, 0, j]]
        for k in range(SLOTS):
            a = blocks[j, k]
            if transpose:
                wt[j, k] = a.T
            target = jnp.where(k < count, target_ids[k, 0, j], -1)
            for b in range(NB):
                lhs[pl.ds(b * BLK, BLK), pl.ds(k * BLK, BLK)] = jnp.where(
                    target == b, a, jnp.zeros_like(a)
                )

    def relay_forward(t):
        kappa, idx = t // 8, lax.rem(t, 8)
        other = jnp.logical_or(idx == 1, idx >= 5)
        hh = jnp.where(other, 1 - yh, yh)
        off = jnp.where(
            idx <= 1, 0,
            jnp.where(
                jnp.logical_or(idx == 2, idx == 5), 3,
                jnp.where(jnp.logical_or(idx == 3, idx == 6), 1, 2),
            ),
        )
        xs = lax.rem(x + off, 4)
        piece = rbuf.at[kappa, hh, xs]

        @pl.when(t > 0)
        def _():
            wait_bytes(piece, r_rz.at[t])

        @pl.when(jnp.logical_and(t > 0, t < 32))
        def _():
            copy_to(piece, rbuf.at[kappa + 1, hh, xs], s_rz.at[t], r_rz.at[t + 8], behind).start()

        @pl.when(t == 1)
        def _():
            for n, (target, at) in enumerate(((right, 5), (left, 6), (opposite, 7))):
                copy_to(
                    rbuf.at[0, 1 - yh, x], rbuf.at[0, 1 - yh, x], s_src.at[4 + n], r_rz.at[at], target
                ).start()

        cl = lax.rem(kappa, 2)
        for n in range(2):
            near_n = near(4 * hh + xs, 4 * n + x, 1 - lo)
            role_n = jnp.where(kappa == 2, near_n, kappa // 3)
            skip = jnp.logical_or(
                jnp.logical_and(kappa == 0, near_n == 0), jnp.logical_and(kappa == 4, near_n == 1)
            )

            @pl.when(jnp.logical_not(skip))
            def _(n=n, role_n=role_n):
                copy_to(
                    piece, xbuf.at[cl, hh, xs, share], s_y.at[n * 32 + lax.rem(t, 32)],
                    r_y.at[cl * 8 + hh * 4 + xs], dev(z, n, x, 1 - lo, role_n),
                ).start()

    def forward_panel(c):
        cl = jnp.where(c < 8, 1, 0)
        m = lax.rem(c, 8)
        hh = jnp.where(lax.rem(m, 2) == 0, yh, 1 - yh)
        n = m // 2
        xs = lax.rem(x + jnp.where(n == 0, 0, jnp.where(n == 1, 3, jnp.where(n == 2, 1, 2))), 4)
        wait_bytes(xbuf.at[cl, hh, xs, pl.ds(AR, 4 * RB)], r_y.at[cl * 8 + hh * 4 + xs])
        for b in range(NB):
            stage[b] = xbuf[cl, hh, xs, pl.ds(b * BLK, BLK), :]
        fill(block_of(cl, 4 * hh + xs), wv, stage, cols_s, rows_s, True)
        acc[...] += jnp.dot(lhs[...], rhs[...], preferred_element_type=F32)

    def got_z0(o, hh):
        wait_recv(zbuf.at[0, hh], r_z0[o])
        start(zbuf.at[0, hh], xbuf.at[1, hh, x, arows], r_z1[o], ahead, role_cond=far_role if o == 0 else None)
        comp_direct(o, hh, 0, zbuf.at[0, hh], far_role if o == 0 else None)

    def got_z1(o, hh):
        mine = xbuf.at[1, hh, x, arows]
        wait_recv(mine, r_z1[o])
        start(mine, zbuf.at[1, hh], r_z2[o], ahead)
        start(mine, mine, r_dir[1][o][0], right)
        start(mine, mine, r_dir[1][o][1], left)

    def got_z2(o, hh):
        wait_recv(zbuf.at[1, hh], r_z2[o])
        start(zbuf.at[1, hh], zbuf.at[0, hh], r_z0[o], mate, role_cond=near_role)
        comp_direct(o, hh, 1, zbuf.at[1, hh])
        own = near(4 * hh + x, w)
        xbuf[0, hh, x, arows, :] = zbuf[1 - own, hh]

    def pass_opposite(cl, o, hh):
        from_left, from_right = xbuf.at[cl, hh, xl], xbuf.at[cl, hh, xr]
        whole = cl == 0 and o == 0
        cond = inner if whole else None
        part_l, part_r = (arows, arows) if whole else (low, high)
        wait_recv(from_left.at[arows], r_dir[cl][o][0])
        start(from_left.at[part_l], from_left.at[part_l], r_opp[cl][o][0], right, cond=cond)
        wait_recv(from_right.at[arows], r_dir[cl][o][1])
        start(
            from_right.at[part_r], from_right.at[part_r], r_opp[cl][o][0 if whole else 1], left, cond=cond
        )

    def wait_opposite(cl, o, hh):
        if cl == 0 and o == 0:
            wait_recv(xbuf.at[cl, hh, xo, arows], r_opp[cl][o][0])
        else:
            wait_recv(xbuf.at[cl, hh, xo, low], r_opp[cl][o][0])
            wait_recv(xbuf.at[cl, hh, xo, high], r_opp[cl][o][1])

    def by_role(near_at, far_at):
        return jnp.where(near_role, near_at, far_at)

    events = [
        (-1, 15, lambda: got_z0(0, yh)),
        (7, 17, lambda: got_z0(1, 1 - yh)),
        (7, 19, lambda: got_z1(0, yh)),
        (11, 22, lambda: got_z1(1, 1 - yh)),
        (13, 24, lambda: got_z2(0, yh)),
        (16, 27, lambda: got_z2(1, 1 - yh)),
        (14, 28, lambda: pass_opposite(1, 0, yh)),
        (18, 31, lambda: pass_opposite(1, 1, 1 - yh)),
        (20, 33, lambda: pass_opposite(0, 0, yh)),
        (23, 36, lambda: pass_opposite(0, 1, 1 - yh)),
        (24, 35, lambda: wait_opposite(1, 0, yh)),
        (25, 36, lambda: wait_opposite(1, 1, 1 - yh)),
        (32, 43, lambda: wait_opposite(0, 0, yh)),
        (33, 44, lambda: wait_opposite(0, 1, 1 - yh)),
    ]
    compute_from = by_role(18, 29)

    def forward_step(t, carry):
        for near_at, far_at, what in events:
            pl.when(t == by_role(near_at, far_at))(what)

        @pl.when(t < 40)
        def _():
            relay_forward(t)

        c = t - compute_from

        @pl.when(jnp.logical_and(c >= 0, c < 16))
        def _():
            forward_panel(c)

        return carry

    lax.fori_loop(0, FWD_STEPS, forward_step, 0)

    mid_src[...] = acc[...].astype(BF16)
    r_mid, r_sc = recv_slot(4), recv_slot(4)
    peers = [lax.rem(r + n, 4) for n in range(1, 4)]
    for peer in peers:
        start(mid_src.at[pl.ds(pl.multiple_of(peer * QR, QR), QR)], mid_in.at[r], r_mid + r, (i, peer))
    own_rows = pl.ds(pl.multiple_of(r * QR, QR), QR)
    total = acc[own_rows, :]
    f_own = feat[own_rows, :]
    divisor = dcol[own_rows, :]
    preact = jnp.dot(f_own, wself[...], preferred_element_type=F32) + bias[...].astype(F32)
    load_cot.wait()
    for peer in peers:
        wait_recv(mid_in.at[peer], r_mid + peer)
        total = total + mid_in[peer].astype(F32)
    neighbours = (total / divisor).astype(BF16)
    preact = preact + jnp.dot(neighbours, wneigh[...], preferred_element_type=F32)
    sig = jax.nn.sigmoid(preact)
    slope = sig * (1.0 + preact * (1.0 - sig))
    pre_grad = (cot[...].astype(F32) * slope).astype(BF16)
    contract = (((1,), (1,)), ((), ()))
    scaled = lax.dot_general(pre_grad, wneigh[...], contract, preferred_element_type=F32)
    sbuf[own_rows, :] = (scaled / divisor).astype(BF16)
    for peer in peers:
        start(sbuf.at[own_rows], sbuf.at[own_rows], r_sc + r, (i, peer))
    out[...] = (preact * sig).astype(BF16)
    base[...] = lax.dot_general(pre_grad, wself[...], contract, preferred_element_type=F32)
    for peer in peers:
        wait_recv(sbuf.at[pl.ds(pl.multiple_of(peer * QR, QR), QR)], r_sc + peer)
    for b in range(NB):
        sstage[b] = sbuf[pl.ds(b * BLK, BLK), :]

    b_opp = [[recv_slot(2) for o in range(2)] for cl in range(2)]
    b_dir = [[[recv_slot() for _ in range(2)] for _ in order] for _ in range(2)]
    b_chain = [[recv_slot() for _ in order] for _ in range(3)]
    r_fa = recv_slot(4)
    mine = 2 * lo + yh
    far_opp_side = jnp.where(x <= 1, 0, 1)
    far_opp_to = dev(z, yh, jnp.where(x <= 1, xr, xl), lo, role)

    def backward_panel(c):
        cl = jnp.where(c < 8, 0, 1)
        m = lax.rem(c, 8)
        hh, n = lax.rem(m, 2), m // 2
        xs = lax.rem(x + jnp.where(n == 0, 2, jnp.where(n == 1, 3, jnp.where(n == 2, 1, 0))), 4)
        fill(block_of(cl, 4 * hh + xs), wt, sstage, rows_s, cols_s, False)
        pbuf[cl, hh, xs] = jnp.dot(lhs[...], rhs[...], preferred_element_type=F32).astype(BF16)
        at = cl * 8 + hh * 4 + xs
        for q in range(4):
            copy_to(
                pbuf.at[cl, hh, xs, pl.ds(AR + RB * q, RB)], rin.at[yh, role, cl, hh, xs],
                s_p.at[at * 4 + q], r_p.at[(yh * 2 + role) * 16 + at],
                dev(z, q // 2, x, 1 - lo, q % 2),
            ).start()

    def relay_backward(u):
        kappa, idx = 4 - u // 8, lax.rem(u, 8)
        hh, n = lax.rem(idx, 2), idx // 2
        xs = lax.rem(x + jnp.where(n == 0, 2, jnp.where(n == 1, 3, jnp.where(n == 2, 1, 0))), 4)
        cl = lax.rem(kappa, 2)
        tacc[...] = jnp.zeros_like(tacc)
        for n in range(2):
            near_n = near(4 * hh + xs, 4 * n + x, 1 - lo)
            role_n = jnp.where(kappa == 2, near_n, kappa // 3)
            skip = jnp.logical_or(
                jnp.logical_and(kappa == 0, near_n == 0), jnp.logical_and(kappa == 4, near_n == 1)
            )

            @pl.when(jnp.logical_not(skip))
            def _(n=n, role_n=role_n):
                wait_bytes(
                    rin.at[n, role_n, cl, hh, xs], r_p.at[(n * 2 + role_n) * 16 + cl * 8 + hh * 4 + xs]
                )
                tacc[...] += rin[n, role_n, cl, hh, xs].astype(F32)

        @pl.when(u >= 8)
        def _():
            wait_bytes(tin.at[kappa, hh, xs], r_t.at[u - 8])
            tacc[...] += tin[kappa, hh, xs].astype(F32)

        tout[kappa, hh, xs] = tacc[...].astype(BF16)

        @pl.when(u < 32)
        def _():
            copy_to(tout.at[kappa, hh, xs], tin.at[kappa - 1, hh, xs], s_t.at[u], r_t.at[u], ahead).start()

        @pl.when(u >= 32)
        def _():
            final_relay(idx, hh, xs, True)

    def final_relay(idx, hh, xs, begin):
        source = lo * 4 + x
        for q in range(4):
            for part, (a, rows, quarter, at) in enumerate(B_PARTS[q]):
                here = jnp.logical_and(
                    jnp.logical_and(hh == yh, xs == x), jnp.logical_and(r == quarter, relay == q)
                )
                gone = jnp.logical_and(relay == q, jnp.logical_not(here))
                src, dst = tout.at[0, hh, xs, pl.ds(a, rows)], fin_b.at[source, pl.ds(at, rows)]
                send_sem = s_fb.at[idx * 2 + part]
                if begin:
                    @pl.when(gone)
                    def _(src=src, dst=dst, send_sem=send_sem, quarter=quarter):
                        copy_to(
                            src, dst, send_sem, r_fb.at[source], (z * 8 + hh * 4 + xs, quarter)
                        ).start()

                    @pl.when(here)
                    def _(src=src, dst=dst):
                        pltpu.make_async_copy(src, dst, r_fb.at[source]).start()
                else:
                    @pl.when(gone)
                    def _(src=src, send_sem=send_sem):
                        wait_bytes(src, send_sem)

    def send_opposite(cl):
        for o, hh in enumerate(order):
            if cl == 0 and o == 0:
                start(
                    pbuf.at[cl, hh, xo, arows], opp_in.at[cl, o, far_opp_side],
                    b_opp[cl][o] + far_opp_side, far_opp_to,
                )
            else:
                start(pbuf.at[cl, hh, xo, low], opp_in.at[cl, o, 1, low], b_opp[cl][o] + 1, left)
                start(pbuf.at[cl, hh, xo, high], opp_in.at[cl, o, 0, high], b_opp[cl][o], right)

    def send_direct(cl):
        for o, hh in enumerate(order):
            def merge(side, xs, part, o=o, hh=hh):
                wait_recv(opp_in.at[cl, o, side, part], b_opp[cl][o] + side)
                pbuf[cl, hh, xs, part, :] = (
                    pbuf[cl, hh, xs, part, :].astype(F32) + opp_in[cl, o, side, part, :].astype(F32)
                ).astype(BF16)

            if cl == 0 and o == 0:
                @pl.when(inner)
                def _(merge=merge):
                    merge(0, xr, arows)
                    merge(1, xl, arows)
            else:
                merge(0, xr, high)
                merge(1, xl, low)
            start(pbuf.at[cl, hh, xl, arows], dir_in.at[cl, o, 1], b_dir[cl][o][1], left)
            start(pbuf.at[cl, hh, xr, arows], dir_in.at[cl, o, 0], b_dir[cl][o][0], right)

    def sum_composite(o, hh):
        wait_recv(dir_in.at[0, o, 0], b_dir[0][o][0])
        wait_recv(dir_in.at[0, o, 1], b_dir[0][o][1])
        wp = 4 * hh + x
        n_own = near(wp, w).astype(F32)
        n_left = near(wp, 4 * yh + xl).astype(F32)
        n_right = near(wp, 4 * yh + xr).astype(F32)
        v_own = pbuf[0, hh, x, arows, :].astype(F32)
        v_left = dir_in[0, o, 0].astype(F32)
        v_right = dir_in[0, o, 1].astype(F32)
        znear[o] = n_own * v_own + n_left * v_left + n_right * v_right
        zfar[o] = (1.0 - n_own) * v_own + (1.0 - n_left) * v_left + (1.0 - n_right) * v_right

    def chain_two(o):
        @pl.when(far_role)
        def _():
            chain_out[2, o] = zfar[o].astype(BF16)

        @pl.when(near_role)
        def _():
            wait_recv(chain_in.at[2, o], b_chain[2][o])
            chain_out[2, o] = (zfar[o] + chain_in[2, o].astype(F32)).astype(BF16)

        start(chain_out.at[2, o], chain_in.at[1, o], b_chain[1][o], behind)

    def sum_whole(o, hh):
        wait_recv(dir_in.at[1, o, 0], b_dir[1][o][0])
        wait_recv(dir_in.at[1, o, 1], b_dir[1][o][1])
        zone[o] = (
            pbuf[1, hh, x, arows, :].astype(F32) + dir_in[1, o, 0].astype(F32) + dir_in[1, o, 1].astype(F32)
        )

    def chain_one(o):
        wait_recv(chain_in.at[1, o], b_chain[1][o])
        chain_out[1, o] = (zone[o] + chain_in[1, o].astype(F32)).astype(BF16)
        start(chain_out.at[1, o], chain_in.at[0, o], b_chain[0][o], behind)

    def chain_zero(o, hh):
        wait_recv(chain_in.at[0, o], b_chain[0][o])
        chain_out[0, o] = (znear[o] + chain_in[0, o].astype(F32)).astype(BF16)
        start(chain_out.at[0, o], chain_in.at[2, o], b_chain[2][o], mate, role_cond=far_role)
        for a, rows, quarter, at in A_PARTS:
            src, dst = chain_out.at[0, o, pl.ds(a, rows)], fin_a.at[mine, pl.ds(at, rows)]
            cond = None
            if o == 0:
                cond = not_quarter[quarter]

                @pl.when(jnp.logical_and(near_role, r == quarter))
                def _(src=src, dst=dst):
                    pltpu.make_async_copy(src, dst, recv_sems.at[r_fa + mine]).start()
            start(
                src, dst, r_fa + mine, (z * 8 + hh * 4 + x, quarter), cond=cond, role_cond=near_role
            )

    late = by_role(BWD_LATE, 0)
    back_events = [
        (BWD_LATE + 2, 2, lambda: send_opposite(0)),
        (BWD_LATE + 6, 6, lambda: send_direct(0)),
        (BWD_LATE + 10, 10, lambda: send_opposite(1)),
        (BWD_LATE + 14, 14, lambda: send_direct(1)),
        (BWD_LATE + 13, 12, lambda: sum_composite(0, yh)),
        (BWD_LATE + 15, 13, lambda: sum_composite(1, 1 - yh)),
        (27, 12, lambda: chain_two(0)),
        (29, 13, lambda: chain_two(1)),
        (32, 20, lambda: sum_whole(0, yh)),
        (34, 22, lambda: sum_whole(1, 1 - yh)),
        (32, 20, lambda: chain_one(0)),
        (34, 22, lambda: chain_one(1)),
        (38, 25, lambda: chain_zero(0, yh)),
        (40, 27, lambda: chain_zero(1, 1 - yh)),
    ]

    def backward_step(t, carry):
        for near_at, far_at, what in back_events:
            pl.when(t == by_role(near_at, far_at))(what)

        c = t - late

        @pl.when(jnp.logical_and(c >= 0, c < 16))
        def _():
            backward_panel(c)

        u = t - 2

        @pl.when(jnp.logical_and(u >= 0, u < 40))
        def _():
            relay_backward(u)

        return carry

    lax.fori_loop(0, BWD_STEPS, backward_step, 0)

    for quarter in range(4):
        a_rows = sum(p[1] for p in A_PARTS if p[2] == quarter)

        @pl.when(r == quarter)
        def _(a_rows=a_rows):
            if a_rows:
                part = pl.ds(0, a_rows)
                for source in range(4):
                    wait_recv(fin_a.at[source, part], r_fa + source)
                result = base[part, :]
                for source in range(4):
                    result = result + fin_a[source, part, :].astype(F32)
                grad[part, :] = result.astype(BF16)
            if a_rows < QR:
                part = pl.ds(a_rows, QR - a_rows)
                for source in range(8):
                    wait_bytes(fin_b.at[source, part], r_fb.at[source])
                result = base[part, :]
                for source in range(8):
                    result = result + fin_b[source, part, :].astype(F32)
                grad[part, :] = result.astype(BF16)

    drain()
    drain_many(s_rz, 32, RB)
    drain_many(s_src, 7, RB)
    drain_many(s_y, 64, RB)
    drain_many(s_p, 64, RB)
    drain_many(s_t, 32, RB)

    def drain_final(idx, carry):
        hh, n = lax.rem(idx, 2), idx // 2
        xs = lax.rem(x + jnp.where(n == 0, 2, jnp.where(n == 1, 3, jnp.where(n == 2, 1, 0))), 4)
        final_relay(idx, hh, xs, False)
        return carry

    lax.fori_loop(0, 8, drain_final, 0)


def on_device(
    features, degrees, cotangent, self_weight, neigh_weight, bias_vector,
    block_values, block_rows, block_cols, block_count,
):
    vmem = pl.BlockSpec(memory_space=pltpu.VMEM)
    smem = pl.BlockSpec(memory_space=pltpu.SMEM)
    anyspace = pl.BlockSpec(memory_space=pl.ANY)
    panel = (PR, HID)
    apanel = (AR, HID)
    piece = (RB, HID)
    dma = pltpu.SemaphoreType.DMA
    return pl.pallas_call(
        kernel,
        out_shape=(
            jax.ShapeDtypeStruct((QR, HID), BF16),
            jax.ShapeDtypeStruct((QR, HID), BF16),
        ),
        in_specs=[smem, smem, smem, vmem, vmem, anyspace, vmem, vmem, vmem, anyspace],
        out_specs=(vmem, vmem),
        scratch_shapes=[
            pltpu.VMEM((16, SLOTS, BLK, BLK), BF16),
            pltpu.VMEM((16, SLOTS, BLK, BLK), BF16),
            pltpu.VMEM((2, 2, 4) + panel, BF16),
            pltpu.VMEM((2, 2) + apanel, BF16),
            pltpu.VMEM(panel, F32),
            pltpu.VMEM((PR, SLOTS * BLK), BF16),
            pltpu.VMEM((SLOTS * BLK, HID), BF16),
            pltpu.VMEM((NB, BLK, HID), BF16),
            pltpu.VMEM((NB, BLK, HID), BF16),
            pltpu.VMEM((QR, HID), BF16),
            pltpu.VMEM(panel, F32),
            pltpu.VMEM(panel, BF16),
            pltpu.VMEM((4, QR, HID), BF16),
            pltpu.VMEM(panel, BF16),
            pltpu.VMEM((QR, HID), F32),
            pltpu.VMEM((5, 2, 4) + piece, BF16),
            pltpu.VMEM((2, 2, 4) + panel, BF16),
            pltpu.VMEM((2, 2, 2) + apanel, BF16),
            pltpu.VMEM((2, 2, 2) + apanel, BF16),
            pltpu.VMEM((2,) + apanel, F32),
            pltpu.VMEM((2,) + apanel, F32),
            pltpu.VMEM((2,) + apanel, F32),
            pltpu.VMEM((3, 2) + apanel, BF16),
            pltpu.VMEM((3, 2) + apanel, BF16),
            pltpu.VMEM((4, QR, HID), BF16),
            pltpu.VMEM((2, 2, 2, 2, 4) + piece, BF16),
            pltpu.VMEM((4, 2, 4) + piece, BF16),
            pltpu.VMEM((5, 2, 4) + piece, BF16),
            pltpu.VMEM(piece, F32),
            pltpu.VMEM((8, QR, HID), BF16),
            dma((80,)),
            dma((80,)),
            dma((2,)),
            pltpu.SemaphoreType.REGULAR,
            dma((32,)),
            dma((40,)),
            dma((7,)),
            dma((64,)),
            dma((16,)),
            dma((64,)),
            dma((64,)),
            dma((32,)),
            dma((32,)),
            dma((16,)),
            dma((8,)),
        ],
        compiler_params=pltpu.CompilerParams(
            collective_id=0, has_side_effects=True, vmem_limit_bytes=60 * 1024 * 1024
        ),
        name="sage_layer",
    )(
        jnp.transpose(block_rows, (2, 0, 1)), jnp.transpose(block_cols, (2, 0, 1)), block_count,
        features, degrees.reshape(NB, BLK), cotangent,
        self_weight, neigh_weight, bias_vector[None, :], block_values,
    )


def solution(mesh):
    return jax.shard_map(
        on_device,
        mesh=mesh,
        in_specs=(
            P("rows", None),
            P("rows"),
            P("rows", None),
            P(),
            P(),
            P(),
            P("rows", "rep", None, None, None),
            P("rows", "rep", None),
            P("rows", "rep", None),
            P("rows", "rep"),
        ),
        out_specs=(P(("rows", "rep"), None), P(("rows", "rep"), None)),
        check_vma=False,
    )
```

time: 186 us -> 147 us (0.79)
  Pallas kernels: 176 us -> 142 us
  local copies, waits for them, and re-layouts: 6.53 us -> 4.3 us
  other arithmetic: 1.96 us -> 0 us
    pallas_call x1, Pallas kernels: 176 us -> 142 us  [on_device(): pl.pallas_call(kernel, out_shape=(jax.ShapeDtypeStruct((QR, HID), BF16),...]
    unnamed x4 -> x2, local copies, waits for them, and re-layouts: 5.8 us -> 3.08 us
where the time goes in v2:
time: 147 us
  Pallas kernels  142 us (97%)
  local copies, waits for them, and re-layouts  4.3 us (3%)
    pallas_call x1, Pallas kernels, on_device(): pl.pallas_call(kernel, out_shape=(jax.ShapeDtypeStruct((QR, HID), BF16),...  142 us
    unnamed x2, local copies, waits for them, and re-layouts  3.08 us

profile of v2, /device:TPU:1, one launch (start us, length us, event | category | flops | bytes accessed | tf_op | source)
XLA Modules:
  0.0 146.8 jit_solution(11348803953293210712)
XLA Ops:
  0.6 1.2 broadcast_in_dim.3.bias
  1.9 141.8 %sage_layer.1 = (bf16[192,256]{1,0:T(8,128)(2,1)}, bf16[192,256]{1,0:T(8,128)(2,1)}) custom-call(s32[12,1,16]{2,1,0:T(1,128)} %bitcast.3, s32[12,1,16]{2,1,0:T(1,128)} %bitcast.4, s32[1,16]{1,0:T(1,128)} %cnt_s.1, bf16[768,256]{1,0:T(8,128)(2,1)} %feat.1, s32[6,128]{1,0:T(8,128)} %bitcast.5, bf16[768,256]{1,0:T(8,128)(2,1)} %cot_hbm.1, ...), custom_call_target="tpu_custom_call" | custom-call | tf_op jit(solution)/shard_map/sage_layer/pallas_call | solution.py:635
  143.7 1.5 %copy.14 = bf16[192,256]{1,0:T(8,128)(2,1)} copy(bf16[192,256]{1,0:T(8,128)(2,1)} %get-tuple-element.4) | data formatting | bytes 196608
  145.2 1.5 %copy.15 = bf16[192,256]{1,0:T(8,128)(2,1)} copy(bf16[192,256]{1,0:T(8,128)(2,1)} %get-tuple-element.5) | data formatting | bytes 196608

commit v3 on v2

--- a/solution.py
+++ b/solution.py
@@ -17,9 +17,9 @@
 RB = 80
 AR = PR - 4 * RB
 HA = AR // 2
-FWD_STEPS = 46
-BWD_STEPS = 46
-BWD_LATE = 10
+FWD_STEPS = 47
+BUILD_FROM = 3
+BWD_STEPS = 48
 
 
 def quarter_parts(start, size):
@@ -37,9 +37,9 @@
 
 def kernel(
     rows_s, cols_s, cnt_s, feat, deg, cot_hbm, wself, wneigh, bias, w_hbm,
-    out, grad,
-    wv, wt, xbuf, zbuf, acc, lhs, rhs, stage, sstage, cot, dcol,
-    mid_src, mid_in, sbuf, base, rbuf,
+    both,
+    wv, dense, merged, xbuf, zbuf, acc, cot, dcol,
+    mid_src, mid_in, sbuf, sflip, base, rbuf,
     pbuf, opp_in, dir_in, znear, zfar, zone, chain_in, chain_out, fin_a,
     rin, tin, tout, tacc, fin_b,
     send_sems, recv_sems, load_sems, go_sem,
@@ -158,30 +158,37 @@
         [near(4 * hh + x, 4 * yh + nx) == 0 for nx in (xr, xl)] for hh in order
     ]
 
-    r_z0 = [recv_slot() for _ in order]
-    r_z1 = [recv_slot() for _ in order]
-    r_z2 = [recv_slot() for _ in order]
-    r_dir = [[[recv_slot() for _ in range(2)] for _ in order] for _ in range(2)]
-    r_opp = [[[recv_slot() for _ in range(2)] for _ in order] for _ in range(2)]
-    comp_slots = [[None, None], [None, None]]
-
-    def comp_direct(o, hh, idx, src, role_cond=None):
+    halves = (low, high)
+
+    def slots_for(*counts):
+        if not counts:
+            return recv_slot()
+        return [slots_for(*counts[1:]) for _ in range(counts[0])]
+
+    r_z0, r_z1, r_z2 = slots_for(2, 2), slots_for(2, 2), slots_for(2, 2)
+    r_dir = slots_for(2, 2, 2, 2)
+    r_opp = slots_for(2, 2, 2)
+    comp_slots = [[[None, None], [None, None]], [[None, None], [None, None]]]
+
+    def comp_direct(o, s, hh, idx, src, role_cond=None):
         flags = near_side if idx == 0 else far_side
         for side, target in enumerate((right, left)):
-            comp_slots[o][side] = start(
-                src, xbuf.at[0, hh, x, arows], r_dir[0][o][side], target,
-                cond=flags[o][side], role_cond=role_cond, send_slot=comp_slots[o][side],
+            comp_slots[o][s][side] = start(
+                src, xbuf.at[0, hh, x, halves[s]], r_dir[0][o][s][side], target,
+                cond=flags[o][side], role_cond=role_cond, send_slot=comp_slots[o][s][side],
             )
 
-    own_a = feat.at[arows]
-    start(own_a, xbuf.at[1, yh, x, arows], r_z1[0], ahead, role_cond=near_role)
-    start(own_a, zbuf.at[0, yh], r_z0[1], across, role_cond=near_role)
     own_b = feat.at[share]
     copy_to(own_b, rbuf.at[1, yh, x], s_rz.at[0], r_rz.at[8], behind).start()
     copy_to(feat.at[share_across], rbuf.at[0, yh, x], s_src.at[0], r_rz.at[1], across).start()
     for n, (target, at) in enumerate(((right, 2), (left, 3), (opposite, 4))):
         copy_to(own_b, rbuf.at[0, yh, x], s_src.at[1 + n], r_rz.at[at], target).start()
-    comp_direct(0, yh, 0, own_a, near_role)
+    for s, half in enumerate(halves):
+        start(feat.at[half], xbuf.at[1, yh, x, half], r_z1[0][s], ahead, role_cond=near_role)
+    for s, half in enumerate(halves):
+        start(feat.at[half], zbuf.at[0, yh, half], r_z0[1][s], across, role_cond=near_role)
+    for s, half in enumerate(halves):
+        comp_direct(0, s, yh, 0, feat.at[half], near_role)
 
     @pl.when(near_role)
     def _():
@@ -195,24 +202,38 @@
         dcol[pl.ds(b * BLK, BLK), :] = jnp.broadcast_to(dcol_t[:, b : b + 1], (BLK, HID))
 
     acc[...] = jnp.zeros_like(acc)
-    load_w.wait()
+    merged[SLOTS] = jnp.zeros((BLK, BLK), BF16)
 
     def block_of(cl, wp):
         return jnp.where(cl == 1, 8 + w - wp, lax.rem(w - wp + 16, 16))
 
-    def fill(j, blocks, src, source_ids, target_ids, transpose):
+    def build(c):
+        cl, hh, xs = forward_place(c)
+        wp = 4 * hh + xs
+        j = block_of(cl, wp)
         count = cnt_s[0, j]
+        places = [
+            jnp.where(k < count, rows_s[k, 0, j] * NB + cols_s[k, 0, j], -1) for k in range(SLOTS)
+        ]
         for k in range(SLOTS):
-            rhs[pl.ds(k * BLK, BLK), :] = src[source_ids[k, 0, j]]
-        for k in range(SLOTS):
-            a = blocks[j, k]
-            if transpose:
-                wt[j, k] = a.T
-            target = jnp.where(k < count, target_ids[k, 0, j], -1)
-            for b in range(NB):
-                lhs[pl.ds(b * BLK, BLK), pl.ds(k * BLK, BLK)] = jnp.where(
-                    target == b, a, jnp.zeros_like(a)
-                )
+            before = SLOTS
+            for earlier in range(k):
+                before = jnp.where(places[earlier] == places[k], earlier, before)
+            merged[k] = wv[j, k] if k == 0 else wv[j, k] + merged[before]
+        for b in range(NB):
+            for a in range(NB):
+                last = SLOTS
+                for k in range(SLOTS):
+                    last = jnp.where(places[k] == b * NB + a, k, last)
+                dense[cl * 8 + wp, pl.ds(b * BLK, BLK), pl.ds(a * BLK, BLK)] = merged[last]
+
+    def forward_place(c):
+        cl = jnp.where(c < 8, 1, 0)
+        m = lax.rem(c, 8)
+        hh = jnp.where(lax.rem(m, 2) == 0, yh, 1 - yh)
+        n = m // 2
+        xs = lax.rem(x + jnp.where(n == 0, 0, jnp.where(n == 1, 3, jnp.where(n == 2, 1, 2))), 4)
+        return cl, hh, xs
 
     def relay_forward(t):
         kappa, idx = t // 8, lax.rem(t, 8)
@@ -259,75 +280,79 @@
                 ).start()
 
     def forward_panel(c):
-        cl = jnp.where(c < 8, 1, 0)
-        m = lax.rem(c, 8)
-        hh = jnp.where(lax.rem(m, 2) == 0, yh, 1 - yh)
-        n = m // 2
-        xs = lax.rem(x + jnp.where(n == 0, 0, jnp.where(n == 1, 3, jnp.where(n == 2, 1, 2))), 4)
-        wait_bytes(xbuf.at[cl, hh, xs, pl.ds(AR, 4 * RB)], r_y.at[cl * 8 + hh * 4 + xs])
-        for b in range(NB):
-            stage[b] = xbuf[cl, hh, xs, pl.ds(b * BLK, BLK), :]
-        fill(block_of(cl, 4 * hh + xs), wv, stage, cols_s, rows_s, True)
-        acc[...] += jnp.dot(lhs[...], rhs[...], preferred_element_type=F32)
-
-    def got_z0(o, hh):
-        wait_recv(zbuf.at[0, hh], r_z0[o])
-        start(zbuf.at[0, hh], xbuf.at[1, hh, x, arows], r_z1[o], ahead, role_cond=far_role if o == 0 else None)
-        comp_direct(o, hh, 0, zbuf.at[0, hh], far_role if o == 0 else None)
-
-    def got_z1(o, hh):
-        mine = xbuf.at[1, hh, x, arows]
-        wait_recv(mine, r_z1[o])
-        start(mine, zbuf.at[1, hh], r_z2[o], ahead)
-        start(mine, mine, r_dir[1][o][0], right)
-        start(mine, mine, r_dir[1][o][1], left)
-
-    def got_z2(o, hh):
-        wait_recv(zbuf.at[1, hh], r_z2[o])
-        start(zbuf.at[1, hh], zbuf.at[0, hh], r_z0[o], mate, role_cond=near_role)
-        comp_direct(o, hh, 1, zbuf.at[1, hh])
+        cl, hh, xs = forward_place(c)
+        at = cl * 8 + hh * 4 + xs
+        wait_bytes(xbuf.at[cl, hh, xs, pl.ds(AR, 4 * RB)], r_y.at[at])
+        acc[...] += jnp.dot(dense[at], xbuf[cl, hh, xs], preferred_element_type=F32)
+
+    def got_z0(o, s, hh):
+        piece = zbuf.at[0, hh, halves[s]]
+        role_cond = far_role if o == 0 else None
+        wait_recv(piece, r_z0[o][s])
+        start(piece, xbuf.at[1, hh, x, halves[s]], r_z1[o][s], ahead, role_cond=role_cond)
+        comp_direct(o, s, hh, 0, piece, role_cond)
+
+    def got_z1(o, s, hh):
+        piece = xbuf.at[1, hh, x, halves[s]]
+        wait_recv(piece, r_z1[o][s])
+        start(piece, zbuf.at[1, hh, halves[s]], r_z2[o][s], ahead)
+        start(piece, piece, r_dir[1][o][s][0], right)
+        start(piece, piece, r_dir[1][o][s][1], left)
+
+    def got_z2(o, s, hh):
+        piece = zbuf.at[1, hh, halves[s]]
+        wait_recv(piece, r_z2[o][s])
+        start(piece, zbuf.at[0, hh, halves[s]], r_z0[o][s], mate, role_cond=near_role)
+        comp_direct(o, s, hh, 1, piece)
         own = near(4 * hh + x, w)
-        xbuf[0, hh, x, arows, :] = zbuf[1 - own, hh]
-
-    def pass_opposite(cl, o, hh):
-        from_left, from_right = xbuf.at[cl, hh, xl], xbuf.at[cl, hh, xr]
+        xbuf[0, hh, x, halves[s], :] = zbuf[1 - own, hh, halves[s], :]
+
+    def pass_opposite(cl, o, s, hh):
         whole = cl == 0 and o == 0
         cond = inner if whole else None
-        part_l, part_r = (arows, arows) if whole else (low, high)
-        wait_recv(from_left.at[arows], r_dir[cl][o][0])
-        start(from_left.at[part_l], from_left.at[part_l], r_opp[cl][o][0], right, cond=cond)
-        wait_recv(from_right.at[arows], r_dir[cl][o][1])
-        start(
-            from_right.at[part_r], from_right.at[part_r], r_opp[cl][o][0 if whole else 1], left, cond=cond
-        )
-
-    def wait_opposite(cl, o, hh):
-        if cl == 0 and o == 0:
-            wait_recv(xbuf.at[cl, hh, xo, arows], r_opp[cl][o][0])
-        else:
-            wait_recv(xbuf.at[cl, hh, xo, low], r_opp[cl][o][0])
-            wait_recv(xbuf.at[cl, hh, xo, high], r_opp[cl][o][1])
+        for side, (xs, target) in enumerate(((xl, right), (xr, left))):
+            piece = xbuf.at[cl, hh, xs, halves[s]]
+            wait_recv(piece, r_dir[cl][o][s][side])
+            if whole or s == side:
+                start(piece, piece, r_opp[cl][o][s], target, cond=cond)
+
+    def wait_opposite(cl, o, s, hh):
+        wait_recv(xbuf.at[cl, hh, xo, halves[s]], r_opp[cl][o][s])
 
     def by_role(near_at, far_at):
         return jnp.where(near_role, near_at, far_at)
 
     events = [
-        (-1, 15, lambda: got_z0(0, yh)),
-        (7, 17, lambda: got_z0(1, 1 - yh)),
-        (7, 19, lambda: got_z1(0, yh)),
-        (11, 22, lambda: got_z1(1, 1 - yh)),
-        (13, 24, lambda: got_z2(0, yh)),
-        (16, 27, lambda: got_z2(1, 1 - yh)),
-        (14, 28, lambda: pass_opposite(1, 0, yh)),
-        (18, 31, lambda: pass_opposite(1, 1, 1 - yh)),
-        (20, 33, lambda: pass_opposite(0, 0, yh)),
-        (23, 36, lambda: pass_opposite(0, 1, 1 - yh)),
-        (24, 35, lambda: wait_opposite(1, 0, yh)),
-        (25, 36, lambda: wait_opposite(1, 1, 1 - yh)),
-        (32, 43, lambda: wait_opposite(0, 0, yh)),
-        (33, 44, lambda: wait_opposite(0, 1, 1 - yh)),
+        (-1, 12, lambda: got_z0(0, 0, order[0])),
+        (38, 43, lambda: wait_opposite(0, 1, 1, order[1])),
+        (4, 15, lambda: got_z0(1, 0, order[1])),
+        (4, 17, lambda: got_z0(1, 1, order[1])),
+        (4, 18, lambda: got_z1(0, 0, order[0])),
+        (25, 36, lambda: pass_opposite(0, 1, 1, order[1])),
+        (7, 23, lambda: got_z1(1, 0, order[1])),
+        (14, 27, lambda: got_z2(1, 0, order[1])),
+        (11, 24, lambda: got_z2(0, 0, order[0])),
+        (11, 24, lambda: got_z2(0, 1, order[0])),
+        (9, 23, lambda: got_z1(1, 1, order[1])),
+        (16, 30, lambda: got_z2(1, 1, order[1])),
+        (12, 28, lambda: pass_opposite(1, 0, 0, order[0])),
+        (13, 30, lambda: pass_opposite(1, 0, 1, order[0])),
+        (4, 21, lambda: got_z1(0, 1, order[0])),
+        (17, 32, lambda: pass_opposite(1, 1, 1, order[1])),
+        (29, 37, lambda: wait_opposite(1, 1, 0, order[1])),
+        (16, 30, lambda: pass_opposite(1, 1, 0, order[1])),
+        (24, 39, lambda: pass_opposite(0, 1, 0, order[1])),
+        (19, 35, lambda: pass_opposite(0, 0, 1, order[0])),
+        (23, 36, lambda: wait_opposite(1, 0, 1, order[0])),
+        (24, 35, lambda: wait_opposite(1, 0, 0, order[0])),
+        (28, 33, lambda: pass_opposite(0, 0, 0, order[0])),
+        (26, 37, lambda: wait_opposite(1, 1, 1, order[1])),
+        (35, 39, lambda: wait_opposite(0, 0, 0, order[0])),
+        (-1, 14, lambda: got_z0(0, 1, order[0])),
+        (32, 45, lambda: wait_opposite(0, 1, 0, order[1])),
+        (30, 40, lambda: wait_opposite(0, 0, 1, order[0])),
     ]
-    compute_from = by_role(18, 29)
+    compute_from = by_role(24, 31)
 
     def forward_step(t, carry):
         for near_at, far_at, what in events:
@@ -336,6 +361,14 @@
         @pl.when(t < 40)
         def _():
             relay_forward(t)
+
+        @pl.when(t == BUILD_FROM)
+        def _():
+            load_w.wait()
+
+        @pl.when(jnp.logical_and(t >= BUILD_FROM, t < BUILD_FROM + 16))
+        def _():
+            build(t - BUILD_FROM)
 
         c = t - compute_from
 
@@ -356,7 +389,7 @@
     total = acc[own_rows, :]
     f_own = feat[own_rows, :]
     divisor = dcol[own_rows, :]
-    preact = jnp.dot(f_own, wself[...], preferred_element_type=F32) + bias[...].astype(F32)
+    preact = jnp.dot(f_own, wself[...], preferred_element_type=F32) + bias[...].astype(F32)[None, :]
     load_cot.wait()
     for peer in peers:
         wait_recv(mid_in.at[peer], r_mid + peer)
@@ -371,12 +404,11 @@
     sbuf[own_rows, :] = (scaled / divisor).astype(BF16)
     for peer in peers:
         start(sbuf.at[own_rows], sbuf.at[own_rows], r_sc + r, (i, peer))
-    out[...] = (preact * sig).astype(BF16)
+    both[:, 0:HID] = (preact * sig).astype(BF16)
     base[...] = lax.dot_general(pre_grad, wself[...], contract, preferred_element_type=F32)
     for peer in peers:
         wait_recv(sbuf.at[pl.ds(pl.multiple_of(peer * QR, QR), QR)], r_sc + peer)
-    for b in range(NB):
-        sstage[b] = sbuf[pl.ds(b * BLK, BLK), :]
+    sflip[...] = sbuf[...].T
 
     b_opp = [[recv_slot(2) for o in range(2)] for cl in range(2)]
     b_dir = [[[recv_slot() for _ in range(2)] for _ in order] for _ in range(2)]
@@ -391,9 +423,9 @@
         m = lax.rem(c, 8)
         hh, n = lax.rem(m, 2), m // 2
         xs = lax.rem(x + jnp.where(n == 0, 2, jnp.where(n == 1, 3, jnp.where(n == 2, 1, 0))), 4)
-        fill(block_of(cl, 4 * hh + xs), wt, sstage, rows_s, cols_s, False)
-        pbuf[cl, hh, xs] = jnp.dot(lhs[...], rhs[...], preferred_element_type=F32).astype(BF16)
         at = cl * 8 + hh * 4 + xs
+        flipped = jnp.dot(sflip[...], dense[at], preferred_element_type=F32)
+        pbuf[cl, hh, xs] = flipped.astype(BF16).T
         for q in range(4):
             copy_to(
                 pbuf.at[cl, hh, xs, pl.ds(AR + RB * q, RB)], rin.at[yh, role, cl, hh, xs],
@@ -472,24 +504,23 @@
                 start(pbuf.at[cl, hh, xo, low], opp_in.at[cl, o, 1, low], b_opp[cl][o] + 1, left)
                 start(pbuf.at[cl, hh, xo, high], opp_in.at[cl, o, 0, high], b_opp[cl][o], right)
 
-    def send_direct(cl):
-        for o, hh in enumerate(order):
-            def merge(side, xs, part, o=o, hh=hh):
-                wait_recv(opp_in.at[cl, o, side, part], b_opp[cl][o] + side)
-                pbuf[cl, hh, xs, part, :] = (
-                    pbuf[cl, hh, xs, part, :].astype(F32) + opp_in[cl, o, side, part, :].astype(F32)
-                ).astype(BF16)
-
-            if cl == 0 and o == 0:
-                @pl.when(inner)
-                def _(merge=merge):
-                    merge(0, xr, arows)
-                    merge(1, xl, arows)
-            else:
-                merge(0, xr, high)
-                merge(1, xl, low)
-            start(pbuf.at[cl, hh, xl, arows], dir_in.at[cl, o, 1], b_dir[cl][o][1], left)
-            start(pbuf.at[cl, hh, xr, arows], dir_in.at[cl, o, 0], b_dir[cl][o][0], right)
+    def send_direct(cl, o, hh):
+        def merge(side, xs, part):
+            wait_recv(opp_in.at[cl, o, side, part], b_opp[cl][o] + side)
+            pbuf[cl, hh, xs, part, :] = (
+                pbuf[cl, hh, xs, part, :].astype(F32) + opp_in[cl, o, side, part, :].astype(F32)
+            ).astype(BF16)
+
+        if cl == 0 and o == 0:
+            @pl.when(inner)
+            def _():
+                merge(0, xr, arows)
+                merge(1, xl, arows)
+        else:
+            merge(0, xr, high)
+            merge(1, xl, low)
+        start(pbuf.at[cl, hh, xl, arows], dir_in.at[cl, o, 1], b_dir[cl][o][1], left)
+        start(pbuf.at[cl, hh, xr, arows], dir_in.at[cl, o, 0], b_dir[cl][o][0], right)
 
     def sum_composite(o, hh):
         wait_recv(dir_in.at[0, o, 0], b_dir[0][o][0])
@@ -545,22 +576,25 @@
                 src, dst, r_fa + mine, (z * 8 + hh * 4 + x, quarter), cond=cond, role_cond=near_role
             )
 
-    late = by_role(BWD_LATE, 0)
+    late = by_role(4, 0)
+    relay_from = by_role(2, 8)
     back_events = [
-        (BWD_LATE + 2, 2, lambda: send_opposite(0)),
-        (BWD_LATE + 6, 6, lambda: send_direct(0)),
-        (BWD_LATE + 10, 10, lambda: send_opposite(1)),
-        (BWD_LATE + 14, 14, lambda: send_direct(1)),
-        (BWD_LATE + 13, 12, lambda: sum_composite(0, yh)),
-        (BWD_LATE + 15, 13, lambda: sum_composite(1, 1 - yh)),
-        (27, 12, lambda: chain_two(0)),
-        (29, 13, lambda: chain_two(1)),
-        (32, 20, lambda: sum_whole(0, yh)),
+        (10, 2, lambda: send_opposite(0)),
+        (38, 26, lambda: chain_zero(0, yh)),
+        (16, 10, lambda: send_opposite(1)),
+        (28, 13, lambda: sum_composite(1, 1 - yh)),
+        (30, 17, lambda: sum_whole(0, yh)),
+        (15, 7, lambda: send_direct(0, 0, yh)),
+        (23, 11, lambda: sum_composite(0, yh)),
+        (44, 29, lambda: chain_zero(1, 1 - yh)),
+        (28, 15, lambda: chain_two(1)),
+        (35, 23, lambda: chain_one(1)),
+        (21, 14, lambda: send_direct(1, 0, yh)),
+        (23, 12, lambda: chain_two(0)),
+        (26, 15, lambda: send_direct(1, 1, 1 - yh)),
+        (18, 8, lambda: send_direct(0, 1, 1 - yh)),
         (34, 22, lambda: sum_whole(1, 1 - yh)),
-        (32, 20, lambda: chain_one(0)),
-        (34, 22, lambda: chain_one(1)),
-        (38, 25, lambda: chain_zero(0, yh)),
-        (40, 27, lambda: chain_zero(1, 1 - yh)),
+        (32, 17, lambda: chain_one(0)),
     ]
 
     def backward_step(t, carry):
@@ -573,7 +607,7 @@
         def _():
             backward_panel(c)
 
-        u = t - 2
+        u = t - relay_from
 
         @pl.when(jnp.logical_and(u >= 0, u < 40))
         def _():
@@ -595,7 +629,7 @@
                 result = base[part, :]
                 for source in range(4):
                     result = result + fin_a[source, part, :].astype(F32)
-                grad[part, :] = result.astype(BF16)
+                both[part, HID:] = result.astype(BF16)
             if a_rows < QR:
                 part = pl.ds(a_rows, QR - a_rows)
                 for source in range(8):
@@ -603,7 +637,7 @@
                 result = base[part, :]
                 for source in range(8):
                     result = result + fin_b[source, part, :].astype(F32)
-                grad[part, :] = result.astype(BF16)
+                both[part, HID:] = result.astype(BF16)
 
     drain()
     drain_many(s_rz, 32, RB)
@@ -632,29 +666,24 @@
     apanel = (AR, HID)
     piece = (RB, HID)
     dma = pltpu.SemaphoreType.DMA
-    return pl.pallas_call(
+    both = pl.pallas_call(
         kernel,
-        out_shape=(
-            jax.ShapeDtypeStruct((QR, HID), BF16),
-            jax.ShapeDtypeStruct((QR, HID), BF16),
-        ),
+        out_shape=jax.ShapeDtypeStruct((QR, 2 * HID), BF16),
         in_specs=[smem, smem, smem, vmem, vmem, anyspace, vmem, vmem, vmem, anyspace],
-        out_specs=(vmem, vmem),
+        out_specs=vmem,
         scratch_shapes=[
             pltpu.VMEM((16, SLOTS, BLK, BLK), BF16),
-            pltpu.VMEM((16, SLOTS, BLK, BLK), BF16),
+            pltpu.VMEM((16, PR, PR), BF16),
+            pltpu.VMEM((SLOTS + 1, BLK, BLK), BF16),
             pltpu.VMEM((2, 2, 4) + panel, BF16),
             pltpu.VMEM((2, 2) + apanel, BF16),
             pltpu.VMEM(panel, F32),
-            pltpu.VMEM((PR, SLOTS * BLK), BF16),
-            pltpu.VMEM((SLOTS * BLK, HID), BF16),
-            pltpu.VMEM((NB, BLK, HID), BF16),
-            pltpu.VMEM((NB, BLK, HID), BF16),
             pltpu.VMEM((QR, HID), BF16),
             pltpu.VMEM(panel, F32),
             pltpu.VMEM(panel, BF16),
             pltpu.VMEM((4, QR, HID), BF16),
             pltpu.VMEM(panel, BF16),
+            pltpu.VMEM((HID, PR), BF16),
             pltpu.VMEM((QR, HID), F32),
             pltpu.VMEM((5, 2, 4) + piece, BF16),
             pltpu.VMEM((2, 2, 4) + panel, BF16),
@@ -671,8 +700,8 @@
             pltpu.VMEM((5, 2, 4) + piece, BF16),
             pltpu.VMEM(piece, F32),
             pltpu.VMEM((8, QR, HID), BF16),
-            dma((80,)),
-            dma((80,)),
+            dma((128,)),
+            dma((128,)),
             dma((2,)),
             pltpu.SemaphoreType.REGULAR,
             dma((32,)),
@@ -694,8 +723,9 @@
     )(
         jnp.transpose(block_rows, (2, 0, 1)), jnp.transpose(block_cols, (2, 0, 1)), block_count,
         features, degrees.reshape(NB, BLK), cotangent,
-        self_weight, neigh_weight, bias_vector[None, :], block_values,
+        self_weight, neigh_weight, bias_vector, block_values,
     )
+    return both[:, 0:HID], both[:, HID:]
 
 
 def solution(mesh):

time: 147 us -> 132 us (0.90)
  Pallas kernels: 142 us -> 129 us
  local copies, waits for them, and re-layouts: 4.3 us -> 1.63 us
    pallas_call x1, Pallas kernels: 142 us -> 129 us  [on_device(): pl.pallas_call(kernel, out_shape=jax.ShapeDtypeStruct((QR, 2 * HID), BF16...]
    unnamed x2 -> x0, local copies, waits for them, and re-layouts: 3.08 us -> none
    slice x0 -> x1, local copies, waits for them, and re-layouts: none -> 1.63 us  [on_device(): return (both[:, 0:HID], both[:, HID:])]
where the time goes in v3:
time: 132 us
  Pallas kernels  129 us (98%)
  local copies, waits for them, and re-layouts  1.63 us (1%)
    pallas_call x1, Pallas kernels, on_device(): pl.pallas_call(kernel, out_shape=jax.ShapeDtypeStruct((QR, 2 * HID), BF16...  129 us

profile of v3, /device:TPU:1, one launch (start us, length us, event | category | flops | bytes accessed | tf_op | source)
XLA Modules:
  0.0 131.7 jit_solution(12169631606510336486)
XLA Ops:
  0.6 129.5 %sage_layer.1 = bf16[192,512]{1,0:T(8,128)(2,1)} custom-call(s32[12,1,16]{2,1,0:T(1,128)} %bitcast.3, s32[12,1,16]{2,1,0:T(1,128)} %bitcast.4, s32[1,16]{1,0:T(1,128)} %cnt_s.1, bf16[768,256]{1,0:T(8,128)(2,1)} %feat.1, s32[6,128]{1,0:T(8,128)} %bitcast.5, bf16[768,256]{1,0:T(8,128)(2,1)} %cot_hbm.1, bf16[256,256]{1,0:T(8,128)(2,1)} %wself.1, ...), custom_call_target="tpu_custom_call" | custom-call | tf_op jit(solution)/shard_map/sage_layer/pallas_call | solution.py:669
  130.1 1.6 %fusion = (bf16[192,256]{1,0:T(8,128)(2,1)}, bf16[192,256]{1,0:T(8,128)(2,1)}) fusion(bf16[192,512]{1,0:T(8,128)(2,1)} %sage_layer.1), kind=kLoop, calls=%fused_computation | loop fusion | bytes 393216 | tf_op jit(solution)/shard_map/slice | solution.py:728

commit v4 on v3

--- a/solution.py
+++ b/solution.py
@@ -19,7 +19,7 @@
 HA = AR // 2
 FWD_STEPS = 47
 BUILD_FROM = 3
-BWD_STEPS = 48
+BWD_STEPS = 46
 
 
 def quarter_parts(start, size):
@@ -31,15 +31,15 @@
     return parts
 
 
-A_PARTS = quarter_parts(0, AR)
+A_PARTS = [quarter_parts(0, HA), quarter_parts(HA, HA)]
 B_PARTS = [quarter_parts(AR + q * RB, RB) for q in range(4)]
 
 
 def kernel(
-    rows_s, cols_s, cnt_s, feat, deg, cot_hbm, wself, wneigh, bias, w_hbm,
+    rows_s, cols_s, cnt_s, feat_hbm, deg, cot_hbm, wself_hbm, wneigh_hbm, bias, w_hbm,
     both,
-    wv, dense, merged, xbuf, zbuf, acc, cot, dcol,
-    mid_src, mid_in, sbuf, sflip, base, rbuf,
+    feat, wself, wneigh, wv, dense, merged, xbuf, zbuf, acc, cot, dcol,
+    mid_src, mid_in, mid_out, sbuf, sflip, base, rbuf,
     pbuf, opp_in, dir_in, znear, zfar, zone, chain_in, chain_out, fin_a,
     rin, tin, tout, tacc, fin_b,
     send_sems, recv_sems, load_sems, go_sem,
@@ -71,10 +71,16 @@
     def near(wp, w_at, lo_at=lo):
         return lax.rem(jnp.where(wp <= w_at, 1, 0) + lo_at, 2)
 
+    load_feat = pltpu.make_async_copy(feat_hbm, feat, load_sems.at[2])
+    load_feat.start()
     load_w = pltpu.make_async_copy(w_hbm.at[0], wv, load_sems.at[0])
     load_w.start()
     load_cot = pltpu.make_async_copy(cot_hbm.at[pl.ds(r * QR, QR)], cot, load_sems.at[1])
     load_cot.start()
+    load_self = pltpu.make_async_copy(wself_hbm, wself, load_sems.at[3])
+    load_self.start()
+    load_neigh = pltpu.make_async_copy(wneigh_hbm, wneigh, load_sems.at[4])
+    load_neigh.start()
 
     barrier = pltpu.get_barrier_semaphore()
 
@@ -89,6 +95,7 @@
     pl.semaphore_signal(barrier, inc=1, device_id=ahead, device_id_type=MESH)
     pl.semaphore_signal(barrier, inc=1, device_id=behind, device_id_type=MESH)
     pl.semaphore_wait(barrier, 33)
+    load_feat.wait()
 
     sends, recvs, pending = [0], [0], []
 
@@ -381,19 +388,31 @@
     lax.fori_loop(0, FWD_STEPS, forward_step, 0)
 
     mid_src[...] = acc[...].astype(BF16)
-    r_mid, r_sc = recv_slot(4), recv_slot(4)
-    peers = [lax.rem(r + n, 4) for n in range(1, 4)]
-    for peer in peers:
-        start(mid_src.at[pl.ds(pl.multiple_of(peer * QR, QR), QR)], mid_in.at[r], r_mid + r, (i, peer))
+    r_mid, r_sc = recv_slot(3), recv_slot(3)
+    core_mate, chip_mate = (i, 2 * lo + 1 - core), (i, 2 * (1 - lo) + core)
+
+    def quarter_rows(lo_, core_):
+        return pl.ds(pl.multiple_of((2 * lo_ + core_) * QR, QR), QR)
+
+    for lo_ in (1 - lo, lo):
+        start(mid_src.at[quarter_rows(lo_, 1 - core)], mid_in.at[lo_], r_mid + lo_, core_mate)
+    wait_recv(mid_in.at[1 - lo], r_mid + 1 - lo)
+    mid_out[...] = (
+        acc[quarter_rows(1 - lo, core), :] + mid_in[1 - lo].astype(F32)
+    ).astype(BF16)
+    start(mid_out, mid_in.at[2], r_mid + 2, chip_mate)
     own_rows = pl.ds(pl.multiple_of(r * QR, QR), QR)
+    load_self.wait()
+    load_neigh.wait()
     total = acc[own_rows, :]
     f_own = feat[own_rows, :]
     divisor = dcol[own_rows, :]
     preact = jnp.dot(f_own, wself[...], preferred_element_type=F32) + bias[...].astype(F32)[None, :]
     load_cot.wait()
-    for peer in peers:
-        wait_recv(mid_in.at[peer], r_mid + peer)
-        total = total + mid_in[peer].astype(F32)
+    wait_recv(mid_in.at[lo], r_mid + lo)
+    total = total + mid_in[lo].astype(F32)
+    wait_recv(mid_in.at[2], r_mid + 2)
+    total = total + mid_in[2].astype(F32)
     neighbours = (total / divisor).astype(BF16)
     preact = preact + jnp.dot(neighbours, wneigh[...], preferred_element_type=F32)
     sig = jax.nn.sigmoid(preact)
@@ -402,17 +421,20 @@
     contract = (((1,), (1,)), ((), ()))
     scaled = lax.dot_general(pre_grad, wneigh[...], contract, preferred_element_type=F32)
     sbuf[own_rows, :] = (scaled / divisor).astype(BF16)
-    for peer in peers:
-        start(sbuf.at[own_rows], sbuf.at[own_rows], r_sc + r, (i, peer))
+    start(sbuf.at[own_rows], sbuf.at[own_rows], r_sc, chip_mate)
+    start(sbuf.at[own_rows], sbuf.at[own_rows], r_sc + 1, core_mate)
     both[:, 0:HID] = (preact * sig).astype(BF16)
     base[...] = lax.dot_general(pre_grad, wself[...], contract, preferred_element_type=F32)
-    for peer in peers:
-        wait_recv(sbuf.at[pl.ds(pl.multiple_of(peer * QR, QR), QR)], r_sc + peer)
+    passed_on = sbuf.at[quarter_rows(1 - lo, core)]
+    wait_recv(passed_on, r_sc)
+    start(passed_on, passed_on, r_sc + 2, core_mate)
+    wait_recv(sbuf.at[quarter_rows(lo, 1 - core)], r_sc + 1)
+    wait_recv(sbuf.at[quarter_rows(1 - lo, 1 - core)], r_sc + 2)
     sflip[...] = sbuf[...].T
 
     b_opp = [[recv_slot(2) for o in range(2)] for cl in range(2)]
     b_dir = [[[recv_slot() for _ in range(2)] for _ in order] for _ in range(2)]
-    b_chain = [[recv_slot() for _ in order] for _ in range(3)]
+    b_chain = slots_for(3, 2, 2)
     r_fa = recv_slot(4)
     mine = 2 * lo + yh
     far_opp_side = jnp.where(x <= 1, 0, 1)
@@ -535,17 +557,21 @@
         znear[o] = n_own * v_own + n_left * v_left + n_right * v_right
         zfar[o] = (1.0 - n_own) * v_own + (1.0 - n_left) * v_left + (1.0 - n_right) * v_right
 
-    def chain_two(o):
+    def chain_two(o, s):
+        half = halves[s]
+
         @pl.when(far_role)
         def _():
-            chain_out[2, o] = zfar[o].astype(BF16)
+            chain_out[2, o, half, :] = zfar[o, half, :].astype(BF16)
 
         @pl.when(near_role)
         def _():
-            wait_recv(chain_in.at[2, o], b_chain[2][o])
-            chain_out[2, o] = (zfar[o] + chain_in[2, o].astype(F32)).astype(BF16)
-
-        start(chain_out.at[2, o], chain_in.at[1, o], b_chain[1][o], behind)
+            wait_recv(chain_in.at[2, o, half], b_chain[2][o][s])
+            chain_out[2, o, half, :] = (
+                zfar[o, half, :] + chain_in[2, o, half, :].astype(F32)
+            ).astype(BF16)
+
+        start(chain_out.at[2, o, half], chain_in.at[1, o, half], b_chain[1][o][s], behind)
 
     def sum_whole(o, hh):
         wait_recv(dir_in.at[1, o, 0], b_dir[1][o][0])
@@ -554,17 +580,26 @@
             pbuf[1, hh, x, arows, :].astype(F32) + dir_in[1, o, 0].astype(F32) + dir_in[1, o, 1].astype(F32)
         )
 
-    def chain_one(o):
-        wait_recv(chain_in.at[1, o], b_chain[1][o])
-        chain_out[1, o] = (zone[o] + chain_in[1, o].astype(F32)).astype(BF16)
-        start(chain_out.at[1, o], chain_in.at[0, o], b_chain[0][o], behind)
-
-    def chain_zero(o, hh):
-        wait_recv(chain_in.at[0, o], b_chain[0][o])
-        chain_out[0, o] = (znear[o] + chain_in[0, o].astype(F32)).astype(BF16)
-        start(chain_out.at[0, o], chain_in.at[2, o], b_chain[2][o], mate, role_cond=far_role)
-        for a, rows, quarter, at in A_PARTS:
-            src, dst = chain_out.at[0, o, pl.ds(a, rows)], fin_a.at[mine, pl.ds(at, rows)]
+    def chain_one(o, s):
+        half = halves[s]
+        wait_recv(chain_in.at[1, o, half], b_chain[1][o][s])
+        chain_out[1, o, half, :] = (
+            zone[o, half, :] + chain_in[1, o, half, :].astype(F32)
+        ).astype(BF16)
+        start(chain_out.at[1, o, half], chain_in.at[0, o, half], b_chain[0][o][s], behind)
+
+    def chain_zero(o, s, hh):
+        half = halves[s]
+        wait_recv(chain_in.at[0, o, half], b_chain[0][o][s])
+        chain_out[0, o, half, :] = (
+            znear[o, half, :] + chain_in[0, o, half, :].astype(F32)
+        ).astype(BF16)
+        start(
+            chain_out.at[0, o, half], chain_in.at[2, o, half], b_chain[2][o][s], mate, role_cond=far_role
+        )
+        for a, rows, quarter, at in A_PARTS[s]:
+            src = chain_out.at[0, o, pl.ds(s * HA + a, rows)]
+            dst = fin_a.at[mine, pl.ds(at, rows)]
             cond = None
             if o == 0:
                 cond = not_quarter[quarter]
@@ -576,25 +611,31 @@
                 src, dst, r_fa + mine, (z * 8 + hh * 4 + x, quarter), cond=cond, role_cond=near_role
             )
 
-    late = by_role(4, 0)
-    relay_from = by_role(2, 8)
+    late = by_role(5, 0)
+    relay_from = by_role(2, 6)
     back_events = [
         (10, 2, lambda: send_opposite(0)),
-        (38, 26, lambda: chain_zero(0, yh)),
+        (30, 17, lambda: sum_whole(0, yh)),
+        (38, 26, lambda: chain_zero(0, 1, yh)),
         (16, 10, lambda: send_opposite(1)),
-        (28, 13, lambda: sum_composite(1, 1 - yh)),
-        (30, 17, lambda: sum_whole(0, yh)),
-        (15, 7, lambda: send_direct(0, 0, yh)),
+        (28, 14, lambda: sum_composite(1, 1 - yh)),
+        (37, 24, lambda: chain_zero(0, 0, yh)),
+        (17, 7, lambda: send_direct(0, 0, yh)),
         (23, 11, lambda: sum_composite(0, yh)),
-        (44, 29, lambda: chain_zero(1, 1 - yh)),
-        (28, 15, lambda: chain_two(1)),
-        (35, 23, lambda: chain_one(1)),
-        (21, 14, lambda: send_direct(1, 0, yh)),
-        (23, 12, lambda: chain_two(0)),
-        (26, 15, lambda: send_direct(1, 1, 1 - yh)),
-        (18, 8, lambda: send_direct(0, 1, 1 - yh)),
+        (38, 28, lambda: chain_zero(1, 0, 1 - yh)),
+        (38, 29, lambda: chain_zero(1, 1, 1 - yh)),
+        (28, 16, lambda: chain_two(1, 0)),
+        (28, 15, lambda: chain_two(1, 1)),
+        (35, 23, lambda: chain_one(1, 0)),
+        (35, 24, lambda: chain_one(1, 1)),
+        (19, 8, lambda: send_direct(0, 1, 1 - yh)),
+        (23, 14, lambda: chain_two(0, 0)),
+        (26, 11, lambda: chain_two(0, 1)),
+        (25, 15, lambda: send_direct(1, 1, 1 - yh)),
+        (20, 14, lambda: send_direct(1, 0, yh)),
+        (33, 18, lambda: chain_one(0, 1)),
+        (30, 17, lambda: chain_one(0, 0)),
         (34, 22, lambda: sum_whole(1, 1 - yh)),
-        (32, 17, lambda: chain_one(0)),
     ]
 
     def backward_step(t, carry):
@@ -618,7 +659,7 @@
     lax.fori_loop(0, BWD_STEPS, backward_step, 0)
 
     for quarter in range(4):
-        a_rows = sum(p[1] for p in A_PARTS if p[2] == quarter)
+        a_rows = sum(p[1] for parts in A_PARTS for p in parts if p[2] == quarter)
 
         @pl.when(r == quarter)
         def _(a_rows=a_rows):
@@ -669,9 +710,12 @@
     both = pl.pallas_call(
         kernel,
         out_shape=jax.ShapeDtypeStruct((QR, 2 * HID), BF16),
-        in_specs=[smem, smem, smem, vmem, vmem, anyspace, vmem, vmem, vmem, anyspace],
+        in_specs=[smem, smem, smem, anyspace, vmem, anyspace, anyspace, anyspace, vmem, anyspace],
         out_specs=vmem,
         scratch_shapes=[
+            pltpu.VMEM(panel, BF16),
+            pltpu.VMEM((HID, HID), BF16),
+            pltpu.VMEM((HID, HID), BF16),
             pltpu.VMEM((16, SLOTS, BLK, BLK), BF16),
             pltpu.VMEM((16, PR, PR), BF16),
             pltpu.VMEM((SLOTS + 1, BLK, BLK), BF16),
@@ -681,7 +725,8 @@
             pltpu.VMEM((QR, HID), BF16),
             pltpu.VMEM(panel, F32),
             pltpu.VMEM(panel, BF16),
-            pltpu.VMEM((4, QR, HID), BF16),
+            pltpu.VMEM((3, QR, HID), BF16),
+            pltpu.VMEM((QR, HID), BF16),
             pltpu.VMEM(panel, BF16),
             pltpu.VMEM((HID, PR), BF16),
             pltpu.VMEM((QR, HID), F32),
@@ -702,7 +747,7 @@
             pltpu.VMEM((8, QR, HID), BF16),
             dma((128,)),
             dma((128,)),
-            dma((2,)),
+            dma((5,)),
             pltpu.SemaphoreType.REGULAR,
             dma((32,)),
             dma((40,)),

time: 132 us -> 129 us (0.977)
  Pallas kernels: 129 us -> 127 us
    pallas_call x1, Pallas kernels: 129 us -> 127 us  [on_device(): pl.pallas_call(kernel, out_shape=jax.ShapeDtypeStruct((QR, 2 * HID), BF16...]
where the time goes in v4:
time: 129 us
  Pallas kernels  127 us (98%)
  local copies, waits for them, and re-layouts  1.63 us (1%)
    pallas_call x1, Pallas kernels, on_device(): pl.pallas_call(kernel, out_shape=jax.ShapeDtypeStruct((QR, 2 * HID), BF16...  127 us

profile of v4, /device:TPU:1, one launch (start us, length us, event | category | flops | bytes accessed | tf_op | source)
XLA Modules:
  0.0 128.9 jit_solution(107716402885530966)
XLA Ops:
  0.6 126.6 %sage_layer.1 = bf16[192,512]{1,0:T(8,128)(2,1)} custom-call(s32[12,1,16]{2,1,0:T(1,128)} %bitcast.3, s32[12,1,16]{2,1,0:T(1,128)} %bitcast.4, s32[1,16]{1,0:T(1,128)} %cnt_s.1, bf16[768,256]{1,0:T(8,128)(2,1)} %feat_hbm.1, s32[6,128]{1,0:T(8,128)} %bitcast.5, bf16[768,256]{1,0:T(8,128)(2,1)} %cot_hbm.1, bf16[256,256]{1,0:T(8,128)(2,1)} %wself_hbm.1, ...), custom_call_target="tpu_custom_call" | custom-call | tf_op jit(solution)/shard_map/sage_layer/pallas_call | solution.py:710
  127.2 1.6 %fusion = (bf16[192,256]{1,0:T(8,128)(2,1)}, bf16[192,256]{1,0:T(8,128)(2,1)}) fusion(bf16[192,512]{1,0:T(8,128)(2,1)} %sage_layer.1), kind=kLoop, calls=%fused_computation | loop fusion | bytes 393216 | tf_op jit(solution)/shard_map/slice | solution.py:773

commit v5 on v4

--- a/solution.py
+++ b/solution.py
@@ -206,7 +206,7 @@
     dcol_rows = deg[...].astype(F32)
     dcol_t = jnp.concatenate([dcol_rows, dcol_rows[0:2]], axis=0).T
     for b in range(NB):
-        dcol[pl.ds(b * BLK, BLK), :] = jnp.broadcast_to(dcol_t[:, b : b + 1], (BLK, HID))
+        dcol[pl.ds(b * BLK, BLK), :] = jnp.broadcast_to(dcol_t[:, b : b + 1], (BLK, BLK))
 
     acc[...] = jnp.zeros_like(acc)
     merged[SLOTS] = jnp.zeros((BLK, BLK), BF16)
@@ -286,11 +286,17 @@
                     r_y.at[cl * 8 + hh * 4 + xs], dev(z, n, x, 1 - lo, role_n),
                 ).start()
 
-    def forward_panel(c):
-        cl, hh, xs = forward_place(c)
-        at = cl * 8 + hh * 4 + xs
-        wait_bytes(xbuf.at[cl, hh, xs, pl.ds(AR, 4 * RB)], r_y.at[at])
-        acc[...] += jnp.dot(dense[at], xbuf[cl, hh, xs], preferred_element_type=F32)
+    def forward_pair(c):
+        products = []
+        for panel in (c - 1, c):
+            cl, hh, xs = forward_place(panel)
+            at = cl * 8 + hh * 4 + xs
+            wait_bytes(xbuf.at[cl, hh, xs, pl.ds(AR, 4 * RB)], r_y.at[at])
+            products.append((at, cl, hh, xs))
+        total = acc[...]
+        for at, cl, hh, xs in products:
+            total = total + jnp.dot(dense[at], xbuf[cl, hh, xs], preferred_element_type=F32)
+        acc[...] = total
 
     def got_z0(o, s, hh):
         piece = zbuf.at[0, hh, halves[s]]
@@ -379,9 +385,9 @@
 
         c = t - compute_from
 
-        @pl.when(jnp.logical_and(c >= 0, c < 16))
-        def _():
-            forward_panel(c)
+        @pl.when(jnp.logical_and(jnp.logical_and(c >= 0, c < 16), lax.rem(c, 2) == 1))
+        def _():
+            forward_pair(c)
 
         return carry
 
@@ -406,7 +412,7 @@
     load_neigh.wait()
     total = acc[own_rows, :]
     f_own = feat[own_rows, :]
-    divisor = dcol[own_rows, :]
+    divisor = jnp.concatenate([dcol[own_rows, :], dcol[own_rows, :]], axis=1)
     preact = jnp.dot(f_own, wself[...], preferred_element_type=F32) + bias[...].astype(F32)[None, :]
     load_cot.wait()
     wait_recv(mid_in.at[lo], r_mid + lo)
@@ -723,7 +729,7 @@
             pltpu.VMEM((2, 2) + apanel, BF16),
             pltpu.VMEM(panel, F32),
             pltpu.VMEM((QR, HID), BF16),
-            pltpu.VMEM(panel, F32),
+            pltpu.VMEM((PR, BLK), F32),
             pltpu.VMEM(panel, BF16),
             pltpu.VMEM((3, QR, HID), BF16),
             pltpu.VMEM((QR, HID), BF16),
@@ -762,7 +768,7 @@
             dma((8,)),
         ],
         compiler_params=pltpu.CompilerParams(
-            collective_id=0, has_side_effects=True, vmem_limit_bytes=60 * 1024 * 1024
+            collective_id=0, has_side_effects=True, vmem_limit_bytes=62 * 1024 * 1024
         ),
         name="sage_layer",
     )(

time: 129 us -> 129 us (level)
  no operation moved by 1% of the time
where the time goes in v5:
time: 129 us
  Pallas kernels  127 us (98%)
  local copies, waits for them, and re-layouts  1.63 us (1%)
    pallas_call x1, Pallas kernels, on_device(): pl.pallas_call(kernel, out_shape=jax.ShapeDtypeStruct((QR, 2 * HID), BF16...  127 us

profile of v5, /device:TPU:1, one launch (start us, length us, event | category | flops | bytes accessed | tf_op | source)
XLA Modules:
  0.0 128.9 jit_solution(11374662455343504095)
XLA Ops:
  0.6 126.6 %sage_layer.1 = bf16[192,512]{1,0:T(8,128)(2,1)} custom-call(s32[12,1,16]{2,1,0:T(1,128)} %bitcast.3, s32[12,1,16]{2,1,0:T(1,128)} %bitcast.4, s32[1,16]{1,0:T(1,128)} %cnt_s.1, bf16[768,256]{1,0:T(8,128)(2,1)} %feat_hbm.1, s32[6,128]{1,0:T(8,128)} %bitcast.5, bf16[768,256]{1,0:T(8,128)(2,1)} %cot_hbm.1, bf16[256,256]{1,0:T(8,128)(2,1)} %wself_hbm.1, ...), custom_call_target="tpu_custom_call" | custom-call | tf_op jit(solution)/shard_map/sage_layer/pallas_call | solution.py:716
  127.3 1.6 %fusion = (bf16[192,256]{1,0:T(8,128)(2,1)}, bf16[192,256]{1,0:T(8,128)(2,1)}) fusion(bf16[192,512]{1,0:T(8,128)(2,1)} %sage_layer.1), kind=kLoop, calls=%fused_computation | loop fusion | bytes 393216 | tf_op jit(solution)/shard_map/slice | solution.py:779
